TPU v7x, 128 devices: a whole 4x4x4 slice. The times are simulated.
128 devices in a mesh: sec: 32 (over y_lo, x, z), tile: 4 (over y_hi, core).
Axes of the slice: x: 4, y: 4 (y_hi: 2, y_lo: 2; y = y_hi * 2 + y_lo), z: 4, core: 2. Of those that a mesh axis runs over, the one named last changes fastest.
Arguments:
- displacement: float32 [2, 32, 1024, 2048], P(None, 'sec', 'tile'), may hold values from -6 to 6
- spring: float32 [32, 1024, 2048], P('sec', 'tile'), may hold values from 0.5 to 2
- stiff_table: float32 [8], replicated, may hold values from 0.25 to 2
- match_blocks: int32 [2, 32, 1024], P(None, 'sec', 'tile'), may hold values from 0 to 4095
- match_class: int32 [32, 1024], P('sec', 'tile'), may hold values from 0 to 7
Outputs:
- relaxed: float32 [2, 32, 1024, 2048], P(None, 'sec', 'tile')
All inputs are finite; a program needn't handle non-finite values.
Results may differ from a plain program's by a relative error of at most 0.000053.
Values sent between devices are 32-bit elements; how exact they have to be, the bound alone decides.
A program may use at most 128 MiB of HBM per device.

v0:
```python
import jax
import jax.numpy as jnp
from jax import lax
from jax.sharding import PartitionSpec as P

ITERS = 3


def from_behind(array, axis, by):
    peers = lax.axis_size(axis)
    pairs = [(i, i + by) for i in range(peers) if 0 <= i + by < peers]
    return lax.ppermute(array, axis, pairs)


def with_halo(cells, sides, width):
    for axis, dim in sides:
        count = lax.axis_size(axis)
        ends = count - 1
        head = lax.slice_in_dim(cells, 0, width, axis=dim)
        tail = lax.slice_in_dim(cells, cells.shape[dim] - width, cells.shape[dim], axis=dim)
        cells = jnp.concatenate(
            [
                lax.ppermute(tail, axis, [(i, (i + 1) % count) for i in range(ends)]),
                cells,
                lax.ppermute(head, axis, [((i + 1) % count, i) for i in range(ends)]),
            ],
            axis=dim,
        )
    return cells


def lookup(stiff_table, classes_in):
    levels = jnp.arange(stiff_table.shape[0], dtype=jnp.int32)
    return jnp.sum(
        jnp.where(classes_in[:, None] == levels[None, :], stiff_table[None, :], 0.0), axis=1
    )


def selector(indices, block_count):
    places = jnp.arange(block_count, dtype=jnp.int32)
    return (indices[:, None] == places[None, :]).astype(jnp.float32)


def pick_rows(table, blocked):
    return jnp.einsum(
        "mb,fbc->fmc",
        table,
        blocked,
        precision=lax.Precision.HIGHEST,
        preferred_element_type=jnp.float32,
    )


def spread_rows(table, terms):
    return jnp.einsum(
        "mb,fmc->fbc",
        table,
        terms,
        precision=lax.Precision.HIGHEST,
        preferred_element_type=jnp.float32,
    )


def on_device(displacement, spring, stiff_table, match_blocks, match_class):
    fields, single, height, breadth = displacement.shape
    block_count = height * breadth // 128
    section = lax.axis_index("sec")
    sections = lax.axis_size("sec")
    prev_blocks, prev_class = from_behind((match_blocks, match_class), "sec", 1)
    pick_source = selector(match_blocks[0, 0], block_count)
    pick_target = selector(match_blocks[1, 0], block_count)
    pick_source_before = selector(prev_blocks[0, 0], block_count)
    pick_target_before = selector(prev_blocks[1, 0], block_count)
    coupling = lookup(stiff_table, match_class[0]) * (section < sections - 1).astype(jnp.float32)
    coupling_before = lookup(stiff_table, prev_class[0]) * (section > 0).astype(jnp.float32)
    diag_blocks = jnp.dot(
        coupling, pick_source, precision=lax.Precision.HIGHEST, preferred_element_type=jnp.float32
    )
    diag_blocks = diag_blocks + jnp.dot(
        coupling_before,
        pick_target_before,
        precision=lax.Precision.HIGHEST,
        preferred_element_type=jnp.float32,
    )
    diagonal = 4.0 * spring[0] + jnp.repeat(
        diag_blocks.reshape(height, breadth // 128), 128, axis=1
    )
    field = displacement
    for sweep in range(ITERS):
        blocked = field.reshape(fields, block_count, 128)
        own_source = pick_rows(pick_source, blocked)
        own_target = pick_rows(pick_target_before, blocked)
        above_band = from_behind(field, "sec", -1)
        below_band = from_behind(field, "sec", 1)
        remote_target = pick_rows(pick_target, above_band.reshape(fields, block_count, 128))
        remote_source = pick_rows(pick_source_before, below_band.reshape(fields, block_count, 128))
        term_own = coupling[None, :, None] * (remote_target - own_source)
        term_before = coupling_before[None, :, None] * (remote_source - own_target)
        matched = spread_rows(pick_source, term_own) + spread_rows(pick_target_before, term_before)
        padded = with_halo(field, (("tile", 2),), 1)
        padded = jnp.pad(padded, ((0, 0), (0, 0), (0, 0), (1, 1)))
        laplace = (
            padded[:, :, 2:, 1:-1]
            + padded[:, :, :-2, 1:-1]
            + padded[:, :, 1:-1, 2:]
            + padded[:, :, 1:-1, :-2]
            - 4.0 * field
        )
        force = spring[None] * laplace + matched.reshape(field.shape)
        field = field + 0.8 * force / diagonal[None, None]
    return field


def solution(mesh):
    placed = (
        P(None, "sec", "tile", None),
        P("sec", "tile", None),
        P(),
        P(None, "sec", "tile"),
        P("sec", "tile"),
    )
    return jax.shard_map(
        on_device,
        mesh=mesh,
        in_specs=placed,
        out_specs=P(None, "sec", "tile", None),
        check_vma=False,
    )
```

profile of v0, /device:TPU:97, one launch (start us, length us, event | category | flops | bytes accessed | tf_op | source)
XLA Modules:
  0.0 487.5 jit_solution(7450032936460169635)
XLA Ops:
  2.0 5.4 %collective-permute-start.5 = (f32[2,1,256,2048]{3,2,1,0:T(8,128)}, f32[2,1,256,2048]{3,2,1,0:T(8,128)}, u32[]{:S(2)}, u32[]{:S(2)}) collective-permute-start(f32[2,1,256,2048]{3,2,1,0:T(8,128)} %param.5), channel_id=1, source_target_pairs={{0,4},{4,8},{8,12},{12,16},{16,20},{20,24},{24,28},{28,32},{32,36}... | collective-permute-start | bytes 12582920 | tf_op jit(solution)/shard_map/ppermute | solution.py:12
  12.3 5.9 %collective-permute-start.1 = (f32[2,1,1,2048]{3,2,0,1:T(1,128)S(1)}, f32[2,1,1,2048]{3,2,0,1:T(1,128)S(1)}, u32[]{:S(2)}, u32[]{:S(2)}) collective-permute-start(f32[2,1,1,2048]{3,2,0,1:T(1,128)S(1)} %get-tuple-element.11), channel_id=1, source_target_pairs={{0,1},{1,2},{2,3},{4,5},{5,6},{6,7},{8,9},{9,10},{10,11},{12,13},{... | collective-permute-start | bytes 49160 | tf_op jit(solution)/shard_map/ppermute | solution.py:23
  28.2 68.5 %collective-permute-done.3 = s32[1,256]{1,0:T(1,128)S(1)} collective-permute-done((s32[1,256]{1,0:T(1,128)}, s32[1,256]{1,0:T(1,128)S(1)}, u32[]{:S(2)}, u32[]{:S(2)}) %collective-permute-start.3) | collective-permute-done | bytes 1056 | tf_op jit(solution)/shard_map/ppermute | solution.py:12
  113.2 5.4 %reshape.70 = f32[2,4096,128]{2,1,0:T(8,128)} reshape(f32[2,1,256,2048]{3,2,1,0:T(8,128)} %collective-permute-done.2) | data formatting | bytes 8388608 | tf_op jit(solution)/shard_map/reshape | solution.py:95
  142.0 5.6 %copy.42 = f32[2,4096,128]{2,1,0:T(8,128)} copy(f32[2,4096,128]{1,2,0:T(8,128)} %fusion.2) | data formatting | bytes 8388608 | tf_op jit(solution)/shard_map/add | solution.py:99
  152.5 13.1 %fusion.23 = f32[2,1,256,2048]{3,2,0,1:T(8,128)} fusion(f32[2,1,256,2048]{3,2,0,1:T(8,128)} %bitcast.155, f32[2,1,256,2048]{3,2,0,1:T(8,128)} %reshape.73, f32[2,1,258,2050]{3,2,0,1:T(8,128)} %select_maximum_fusion.4, f32[2,1,1,2048]{3,2,0,1:T(1,128)S(1)} %collective-permute-done.1, f32[2,1,1,2048]{3,2,0,1:T(1,128)S(1)} %collective-permute-done, ...), kind=kLoop, calls=%fused_computation.43 | loop fusion | flops 12582912 | bytes 25198592 | tf_op jit(solution)/shard_map/add | solution.py:110
  167.5 6.2 %collective-permute-start.9 = (f32[2,1,256,2048]{3,2,0,1:T(8,128)}, f32[2,1,256,2048]{3,2,0,1:T(8,128)}, u32[]{:S(2)}, u32[]{:S(2)}) collective-permute-start(f32[2,1,256,2048]{3,2,0,1:T(8,128)} %fusion.23), channel_id=1, source_target_pairs={{0,4},{4,8},{8,12},{12,16},{16,20},{20,24},{24,28},{28,32},{32,36}... | collective-permute-start | bytes 12582920 | tf_op jit(solution)/shard_map/ppermute | solution.py:12
  179.8 5.1 %collective-permute-start.7 = (f32[2,1,1,2048]{3,2,0,1:T(1,128)S(1)}, f32[2,1,1,2048]{3,2,0,1:T(1,128)S(1)}, u32[]{:S(2)}, u32[]{:S(2)}) collective-permute-start(f32[2,1,1,2048]{3,2,0,1:T(1,128)S(1)} %get-tuple-element.9), channel_id=1, source_target_pairs={{0,1},{1,2},{2,3},{4,5},{5,6},{6,7},{8,9},{9,10},{10,11},{12,13},{... | collective-permute-start | bytes 49160 | tf_op jit(solution)/shard_map/ppermute | solution.py:23
  186.8 5.9 %fusion.31 = f32[2,128,256]{2,1,0:T(8,128)S(1)} fusion(f32[2,4096,128]{2,1,0:T(8,128)} %reshape.77, s32[256]{0:T(256)S(1)} %bitcast.171), kind=kOutput, calls=%fused_computation.52 | convolution fusion | flops 3222274048 | bytes 4457472 | tf_op jit(solution)/shard_map/mb,fbc->fmc/dot_general | solution.py:45
  196.5 77.8 %collective-permute-done.6 = f32[2,1,1,2048]{3,2,0,1:T(1,128)S(1)} collective-permute-done((f32[2,1,1,2048]{3,2,0,1:T(1,128)S(1)}, f32[2,1,1,2048]{3,2,0,1:T(1,128)S(1)}, u32[]{:S(2)}, u32[]{:S(2)}) %collective-permute-start.6) | collective-permute-done | bytes 16416 | tf_op jit(solution)/shard_map/ppermute | solution.py:25
  274.4 5.7 %select_maximum_fusion.2 = f32[2,1,258,2050]{3,2,0,1:T(8,128)} fusion(f32[2,1,1,2048]{3,2,0,1:T(1,128)S(1)} %collective-permute-done.6, f32[2,1,256,2048]{3,2,0,1:T(8,128)} %fusion.23, f32[2,1,1,2048]{3,2,0,1:T(1,128)S(1)} %collective-permute-done.7), kind=kLoop, calls=%fused_computation.10 | loop fusion | flops 8462400 | bytes 8458272 | tf_op jit(solution)/shard_map/concatenate | solution.py:21
  285.1 5.9 %fusion.124 = f32[2,256,128]{1,2,0:T(8,128)S(1)} fusion(f32[2,128,256]{2,1,0:T(8,128)S(1)} %fusion.44, f32[2,4096,128]{2,1,0:T(8,128)} %reshape.76, s32[256]{0:T(256)S(1)} %bitcast.180, f32[256]{0:T(256)S(1)} %broadcast_multiply_fusion.1), kind=kOutput, calls=%fused_computation.108 | convolution fusion | flops 3222405120 | bytes 4720640 | tf_op jit(solution)/shard_map/mb,fbc->fmc/dot_general | solution.py:45
  300.3 6.0 %fusion.133 = f32[2,256,128]{1,2,0:T(8,128)S(1)} fusion(f32[2,128,256]{2,1,0:T(8,128)S(1)} %fusion.31, f32[2,4096,128]{2,1,0:T(8,128)} %reshape.78, s32[256]{0:T(256)S(1)} %bitcast.183, f32[256]{0:T(256)S(1)} %broadcast_multiply_fusion), kind=kOutput, calls=%fused_computation.111 | convolution fusion | flops 3222405120 | bytes 4720640 | tf_op jit(solution)/shard_map/mb,fbc->fmc/dot_general | solution.py:45
  310.8 5.6 %copy.48 = f32[2,4096,128]{2,1,0:T(8,128)} copy(f32[2,4096,128]{1,2,0:T(8,128)} %fusion.1) | data formatting | bytes 8388608 | tf_op jit(solution)/shard_map/add | solution.py:99
  321.3 13.1 %fusion.16 = f32[2,1,256,2048]{3,2,0,1:T(8,128)} fusion(f32[2,1,256,2048]{3,2,0,1:T(8,128)} %fusion.23, f32[2,1,256,2048]{3,2,0,1:T(8,128)} %reshape.79, f32[2,1,258,2050]{3,2,0,1:T(8,128)} %select_maximum_fusion.2, f32[2,1,1,2048]{3,2,0,1:T(1,128)S(1)} %collective-permute-done.7, f32[2,1,1,2048]{3,2,0,1:T(1,128)S(1)} %collective-permute-done.6, ...), kind=kLoop, calls=%fused_computation.32 | loop fusion | flops 12582912 | bytes 25198592 | tf_op jit(solution)/shard_map/add | solution.py:110
  336.2 5.5 %collective-permute-start.13 = (f32[2,1,256,2048]{3,2,0,1:T(8,128)}, f32[2,1,256,2048]{3,2,0,1:T(8,128)}, u32[]{:S(2)}, u32[]{:S(2)}) collective-permute-start(f32[2,1,256,2048]{3,2,0,1:T(8,128)} %fusion.16), channel_id=1, source_target_pairs={{0,4},{4,8},{8,12},{12,16},{16,20},{20,24},{24,28},{28,32},{32,36}... | collective-permute-start | bytes 12582920 | tf_op jit(solution)/shard_map/ppermute | solution.py:12
  353.2 5.9 %fusion.28 = f32[2,128,256]{2,1,0:T(8,128)S(1)} fusion(f32[2,4096,128]{2,1,0:T(8,128)} %reshape.81, s32[256]{0:T(256)S(1)} %bitcast.173), kind=kOutput, calls=%fused_computation.51 | convolution fusion | flops 3222274048 | bytes 4457472 | tf_op jit(solution)/shard_map/mb,fbc->fmc/dot_general | solution.py:45
  362.9 64.5 %collective-permute-done.10 = f32[2,1,1,2048]{3,2,0,1:T(1,128)S(1)} collective-permute-done((f32[2,1,1,2048]{3,2,0,1:T(1,128)S(1)}, f32[2,1,1,2048]{3,2,0,1:T(1,128)S(1)}, u32[]{:S(2)}, u32[]{:S(2)}) %collective-permute-start.10) | collective-permute-done | bytes 16416 | tf_op jit(solution)/shard_map/ppermute | solution.py:25
  427.5 5.7 %select_maximum_fusion = f32[2,1,258,2050]{3,2,0,1:T(8,128)} fusion(f32[2,1,1,2048]{3,2,0,1:T(1,128)S(1)} %collective-permute-done.10, f32[2,1,256,2048]{3,2,0,1:T(8,128)} %fusion.16, f32[2,1,1,2048]{3,2,0,1:T(1,128)S(1)} %collective-permute-done.11), kind=kLoop, calls=%fused_computation.8 | loop fusion | flops 8462400 | bytes 8458272 | tf_op jit(solution)/shard_map/concatenate | solution.py:21
  438.2 5.9 %fusion.121 = f32[2,256,128]{1,2,0:T(8,128)S(1)} fusion(f32[2,128,256]{2,1,0:T(8,128)S(1)} %fusion.40, f32[2,4096,128]{2,1,0:T(8,128)} %reshape.80, s32[256]{0:T(256)S(1)} %bitcast.181, f32[256]{0:T(256)S(1)} %broadcast_multiply_fusion.1), kind=kOutput, calls=%fused_computation.107 | convolution fusion | flops 3222405120 | bytes 4720640 | tf_op jit(solution)/shard_map/mb,fbc->fmc/dot_general | solution.py:45
  448.2 5.2 %reshape.82 = f32[2,4096,128]{2,1,0:T(8,128)} reshape(f32[2,1,256,2048]{3,2,0,1:T(8,128)} %collective-permute-done.13) | data formatting | bytes 8388608 | tf_op jit(solution)/shard_map/reshape | solution.py:96
  453.4 6.0 %fusion.130 = f32[2,256,128]{1,2,0:T(8,128)S(1)} fusion(f32[2,128,256]{2,1,0:T(8,128)S(1)} %fusion.28, f32[2,4096,128]{2,1,0:T(8,128)} %reshape.82, s32[256]{0:T(256)S(1)} %bitcast.184, f32[256]{0:T(256)S(1)} %broadcast_multiply_fusion), kind=kOutput, calls=%fused_computation.110 | convolution fusion | flops 3222405120 | bytes 4720640 | tf_op jit(solution)/shard_map/mb,fbc->fmc/dot_general | solution.py:45
  463.8 5.6 %copy.53 = f32[2,4096,128]{2,1,0:T(8,128)} copy(f32[2,4096,128]{1,2,0:T(8,128)} %fusion) | data formatting | bytes 8388608 | tf_op jit(solution)/shard_map/add | solution.py:99
  474.3 13.0 %fusion.50 = f32[2,1,256,2048]{3,2,1,0:T(8,128)} fusion(f32[2,1,256,2048]{3,2,0,1:T(8,128)} %fusion.16, f32[2,1,256,2048]{3,2,0,1:T(8,128)} %reshape.83, f32[2,1,258,2050]{3,2,0,1:T(8,128)} %select_maximum_fusion, f32[2,1,1,2048]{3,2,0,1:T(1,128)S(1)} %collective-permute-done.11, f32[2,1,1,2048]{3,2,0,1:T(1,128)S(1)} %collective-permute-done.10, ...), kind=kLoop, calls=%fused_computation.65 | loop fusion | flops 12582912 | bytes 25198592 | tf_op jit(solution)/shard_map/add | solution.py:110
  (79 shorter events, 134.4 us)
Async XLA Ops:
  0.0 113.2 %collective-permute-start.2 = (f32[2,1,256,2048]{3,2,1,0:T(8,128)}, f32[2,1,256,2048]{3,2,1,0:T(8,128)}, u32[]{:S(2)}, u32[]{:S(2)}) collective-permute-start(f32[2,1,256,2048]{3,2,1,0:T(8,128)} %param.5), channel_id=1, source_target_pairs={{4,0},{8,4},{12,8},{16,12},{20,16},{24,20},{28,24},{32,28},{36,32}... | collective-permute-start | bytes 12582920 | tf_op jit(solution)/shard_map/ppermute | solution.py:12
  2.0 125.6 %collective-permute-start.5 = (f32[2,1,256,2048]{3,2,1,0:T(8,128)}, f32[2,1,256,2048]{3,2,1,0:T(8,128)}, u32[]{:S(2)}, u32[]{:S(2)}) collective-permute-start(f32[2,1,256,2048]{3,2,1,0:T(8,128)} %param.5), channel_id=1, source_target_pairs={{0,4},{4,8},{8,12},{12,16},{16,20},{20,24},{24,28},{28,32},{32,36}... | collective-permute-start | bytes 12582920 | tf_op jit(solution)/shard_map/ppermute | solution.py:12
  7.4 89.2 %collective-permute-start.3 = (s32[1,256]{1,0:T(1,128)}, s32[1,256]{1,0:T(1,128)S(1)}, u32[]{:S(2)}, u32[]{:S(2)}) collective-permute-start(s32[1,256]{1,0:T(1,128)} %param.9), channel_id=1, source_target_pairs={{0,4},{4,8},{8,12},{12,16},{16,20},{20,24},{24,28},{28,32},{32,36}... | collective-permute-start | bytes 3080 | tf_op jit(solution)/shard_map/ppermute | solution.py:12
  9.3 93.0 %collective-permute-start.4 = (s32[2,1,256]{2,1,0:T(1,128)}, s32[2,1,256]{2,1,0:T(1,128)S(1)}, u32[]{:S(2)}, u32[]{:S(2)}) collective-permute-start(s32[2,1,256]{2,1,0:T(1,128)} %param.8), channel_id=1, source_target_pairs={{0,4},{4,8},{8,12},{12,16},{16,20},{20,24},{24,28},{28,32},{32,36}... | collective-permute-start | bytes 6152 | tf_op jit(solution)/shard_map/ppermute | solution.py:12
  12.3 10.9 %copy-start.8 = (s32[2,1,256]{2,1,0:T(1,128)S(1)}, s32[2,1,256]{2,1,0:T(1,128)}, u32[]{:S(2)}) copy-start(s32[2,1,256]{2,1,0:T(1,128)} %param.8) | copy-start | bytes 6148
  12.3 97.4 %collective-permute-start.1 = (f32[2,1,1,2048]{3,2,0,1:T(1,128)S(1)}, f32[2,1,1,2048]{3,2,0,1:T(1,128)S(1)}, u32[]{:S(2)}, u32[]{:S(2)}) collective-permute-start(f32[2,1,1,2048]{3,2,0,1:T(1,128)S(1)} %get-tuple-element.11), channel_id=1, source_target_pairs={{0,1},{1,2},{2,3},{4,5},{5,6},{6,7},{8,9},{9,10},{10,11},{12,13},{... | collective-permute-start | bytes 49160 | tf_op jit(solution)/shard_map/ppermute | solution.py:23
  23.1 77.6 %copy-start.9 = (s32[1,256]{1,0:T(1,128)S(1)}, s32[1,256]{1,0:T(1,128)}, u32[]{:S(2)}) copy-start(s32[1,256]{1,0:T(1,128)} %param.9) | copy-start | bytes 3076
  23.1 77.6 %copy-start.10 = (f32[8]{0:T(128)S(1)}, f32[8]{0:T(128)}, u32[]{:S(2)}) copy-start(f32[8]{0:T(128)} %param.7) | copy-start | bytes 100
  23.1 81.4 %copy-start.4 = (f32[1,256,2048]{2,1,0:T(8,128)S(1)}, f32[1,256,2048]{2,1,0:T(8,128)}, u32[]{:S(2)}) copy-start(f32[1,256,2048]{2,1,0:T(8,128)} %param.6) | copy-start | bytes 6291460
  96.6 13.1 %collective-permute-start = (f32[2,1,1,2048]{3,2,0,1:T(1,128)S(1)}, f32[2,1,1,2048]{3,2,0,1:T(1,128)S(1)}, u32[]{:S(2)}, u32[]{:S(2)}) collective-permute-start(f32[2,1,1,2048]{3,2,0,1:T(1,128)S(1)} %get-tuple-element.12), channel_id=1, source_target_pairs={{1,0},{2,1},{3,2},{5,4},{6,5},{7,6},{9,8},{10,9},{11,10},{13,12},{... | collective-permute-start | bytes 49160 | tf_op jit(solution)/shard_map/ppermute | solution.py:25
  104.5 5.2 %copy-start = (f32[2,1,256,2048]{3,2,1,0:T(8,128)S(1)}, f32[2,1,256,2048]{3,2,1,0:T(8,128)}, u32[]{:S(2)}) copy-start(f32[2,1,256,2048]{3,2,1,0:T(8,128)} %param.5) | copy-start | bytes 12582916
  132.6 5.0 %copy-start.6 = (f32[2,128,4096]{2,1,0:T(8,128)S(1)}, f32[2,128,4096]{2,1,0:T(8,128)}, u32[]{:S(2)}) copy-start(f32[2,128,4096]{2,1,0:T(8,128)} %fusion.46) | copy-start | bytes 12582916
  165.6 114.5 %collective-permute-start.8 = (f32[2,1,256,2048]{3,2,0,1:T(8,128)}, f32[2,1,256,2048]{3,2,0,1:T(8,128)}, u32[]{:S(2)}, u32[]{:S(2)}) collective-permute-start(f32[2,1,256,2048]{3,2,0,1:T(8,128)} %fusion.23), channel_id=1, source_target_pairs={{4,0},{8,4},{12,8},{16,12},{20,16},{24,20},{28,24},{32,28},{36,32}... | collective-permute-start | bytes 12582920 | tf_op jit(solution)/shard_map/ppermute | solution.py:12
  167.5 127.7 %collective-permute-start.9 = (f32[2,1,256,2048]{3,2,0,1:T(8,128)}, f32[2,1,256,2048]{3,2,0,1:T(8,128)}, u32[]{:S(2)}, u32[]{:S(2)}) collective-permute-start(f32[2,1,256,2048]{3,2,0,1:T(8,128)} %fusion.23), channel_id=1, source_target_pairs={{0,4},{4,8},{8,12},{12,16},{16,20},{20,24},{24,28},{28,32},{32,36}... | collective-permute-start | bytes 12582920 | tf_op jit(solution)/shard_map/ppermute | solution.py:12
  178.6 14.1 %copy-start.2 = (f32[2,4096,128]{2,1,0:T(8,128)S(1)}, f32[2,4096,128]{2,1,0:T(8,128)}, u32[]{:S(2)}) copy-start(f32[2,4096,128]{2,1,0:T(8,128)} %reshape.77) | copy-start | bytes 12582916
  179.8 16.8 %collective-permute-start.7 = (f32[2,1,1,2048]{3,2,0,1:T(1,128)S(1)}, f32[2,1,1,2048]{3,2,0,1:T(1,128)S(1)}, u32[]{:S(2)}, u32[]{:S(2)}) collective-permute-start(f32[2,1,1,2048]{3,2,0,1:T(1,128)S(1)} %get-tuple-element.9), channel_id=1, source_target_pairs={{0,1},{1,2},{2,3},{4,5},{5,6},{6,7},{8,9},{9,10},{10,11},{12,13},{... | collective-permute-start | bytes 49160 | tf_op jit(solution)/shard_map/ppermute | solution.py:23
  184.9 89.5 %collective-permute-start.6 = (f32[2,1,1,2048]{3,2,0,1:T(1,128)S(1)}, f32[2,1,1,2048]{3,2,0,1:T(1,128)S(1)}, u32[]{:S(2)}, u32[]{:S(2)}) collective-permute-start(f32[2,1,1,2048]{3,2,0,1:T(1,128)S(1)} %get-tuple-element.10), channel_id=1, source_target_pairs={{1,0},{2,1},{3,2},{5,4},{6,5},{7,6},{9,8},{10,9},{11,10},{13,12},{... | collective-permute-start | bytes 49160 | tf_op jit(solution)/shard_map/ppermute | solution.py:25
  300.3 6.0 %copy-start.7 = (f32[2,128,4096]{2,1,0:T(8,128)S(1)}, f32[2,128,4096]{2,1,0:T(8,128)}, u32[]{:S(2)}) copy-start(f32[2,128,4096]{2,1,0:T(8,128)} %fusion.42) | copy-start | bytes 12582916
  334.3 98.8 %collective-permute-start.12 = (f32[2,1,256,2048]{3,2,0,1:T(8,128)}, f32[2,1,256,2048]{3,2,0,1:T(8,128)}, u32[]{:S(2)}, u32[]{:S(2)}) collective-permute-start(f32[2,1,256,2048]{3,2,0,1:T(8,128)} %fusion.16), channel_id=1, source_target_pairs={{4,0},{8,4},{12,8},{16,12},{20,16},{24,20},{28,24},{32,28},{36,32}... | collective-permute-start | bytes 12582920 | tf_op jit(solution)/shard_map/ppermute | solution.py:12
  336.2 112.0 %collective-permute-start.13 = (f32[2,1,256,2048]{3,2,0,1:T(8,128)}, f32[2,1,256,2048]{3,2,0,1:T(8,128)}, u32[]{:S(2)}, u32[]{:S(2)}) collective-permute-start(f32[2,1,256,2048]{3,2,0,1:T(8,128)} %fusion.16), channel_id=1, source_target_pairs={{0,4},{4,8},{8,12},{12,16},{16,20},{20,24},{24,28},{28,32},{32,36}... | collective-permute-start | bytes 12582920 | tf_op jit(solution)/shard_map/ppermute | solution.py:12
  346.6 12.5 %copy-start.3 = (f32[2,4096,128]{2,1,0:T(8,128)S(1)}, f32[2,4096,128]{2,1,0:T(8,128)}, u32[]{:S(2)}) copy-start(f32[2,4096,128]{2,1,0:T(8,128)} %reshape.81) | copy-start | bytes 12582916
  347.8 15.2 %collective-permute-start.11 = (f32[2,1,1,2048]{3,2,0,1:T(1,128)S(1)}, f32[2,1,1,2048]{3,2,0,1:T(1,128)S(1)}, u32[]{:S(2)}, u32[]{:S(2)}) collective-permute-start(f32[2,1,1,2048]{3,2,0,1:T(1,128)S(1)} %get-tuple-element.7), channel_id=1, source_target_pairs={{0,1},{1,2},{2,3},{4,5},{5,6},{6,7},{8,9},{9,10},{10,11},{12,13},{... | collective-permute-start | bytes 49160 | tf_op jit(solution)/shard_map/ppermute | solution.py:23
  350.8 76.6 %collective-permute-start.10 = (f32[2,1,1,2048]{3,2,0,1:T(1,128)S(1)}, f32[2,1,1,2048]{3,2,0,1:T(1,128)S(1)}, u32[]{:S(2)}, u32[]{:S(2)}) collective-permute-start(f32[2,1,1,2048]{3,2,0,1:T(1,128)S(1)} %get-tuple-element.8), channel_id=1, source_target_pairs={{1,0},{2,1},{3,2},{5,4},{6,5},{7,6},{9,8},{10,9},{11,10},{13,12},{... | collective-permute-start | bytes 49160 | tf_op jit(solution)/shard_map/ppermute | solution.py:25
  453.4 6.0 %copy-start.5 = (f32[2,128,4096]{2,1,0:T(8,128)S(1)}, f32[2,128,4096]{2,1,0:T(8,128)}, u32[]{:S(2)}) copy-start(f32[2,128,4096]{2,1,0:T(8,128)} %fusion.38) | copy-start | bytes 12582916
  (1 other events, 3.1 us)
where the time goes:
time: 492 us; the launch traced here: 487 us
  waiting for transfers between devices  211 us (43%)
  matrix products  89.1 us (18%)
  local copies, waits for them, and re-layouts  80.9 us (16%)
  other arithmetic  56.6 us (12%)
  starting transfers between devices  49.3 us (10%)
    ppermute x3, waiting for transfers between devices, with_halo(): lax.ppermute(head, axis, [((i + 1) % count, i) for i in range(ends)])  142 us
    ppermute x8, waiting for transfers between devices, from_behind(): return lax.ppermute(array, axis, pairs)  68.5 us
    dot_general x12, matrix products, pick_rows(): jnp.einsum('mb,fbc->fmc', table, blocked, precision=lax.Precision.HIGHEST...  60.6 us
    add x3, other arithmetic, on_device(): field = field + 0.8 * force / diagonal[None, None]  39.1 us
    ppermute x8, starting transfers between devices, from_behind(): return lax.ppermute(array, axis, pairs)  26.8 us
    dot_general x6, matrix products, spread_rows(): jnp.einsum('mb,fmc->fbc', table, terms, precision=lax.Precision.HIGHEST,...  25.6 us
    add x3, local copies, waits for them, and re-layouts, on_device(): spread_rows(pick_source, term_own)  16.9 us
    reshape x3, local copies, waits for them, and re-layouts, on_device(): above_band.reshape(fields, block_count, 128)  15.5 us
  transfers between devices with their start and end apart: 14, of which 3 were waited for; matrix products, arithmetic and copies ran while one was open for 23% of the time, Pallas kernels for 0%

commit v1 on v0

v1 whole, which is shorter than its diff:
```python
import functools

import jax
import jax.numpy as jnp
from jax import lax
from jax.experimental import pallas as pl
from jax.experimental.pallas import tpu as pltpu
from jax.sharding import PartitionSpec as P

ITERS = 3
LANES = 128
PAD = 8
CHUNKS = 2
STRIP = 64
MESH = pl.DeviceIdType.MESH
F32 = jnp.float32
BF16 = jnp.bfloat16


def split(value):
    high = value.astype(BF16)
    return high, (value - high.astype(F32)).astype(BF16)


def kernel(
    disp, spring, table, blocks, classes, out,
    f_a, f_b, spr, a_ref, g_ref, onehot, pmat,
    own_index, prev_index, own_blocks, prev_blocks, own_class, prev_class,
    block_cols, cmat, gathered_g, gathered_l, sent, received, t_high, t_low,
    edge_out, edge_in,
    load_sem, spring_sem, list_sem, list_send, list_recv,
    row_send, row_recv, edge_send, edge_recv, out_sem,
):
    fields, _, height, breadth = disp.shape
    columns = breadth // LANES
    matches = classes.shape[1]
    part = matches // CHUNKS
    section, sections = lax.axis_index("sec"), lax.axis_size("sec")
    tile, tiles = lax.axis_index("tile"), lax.axis_size("tile")
    following = lax.rem(section + 1, sections)
    previous = lax.rem(section + sections - 1, sections)
    has_upper, has_lower = tile > 0, tile < tiles - 1

    barrier = pltpu.get_barrier_semaphore()
    for peer in (following, previous):
        pl.semaphore_signal(barrier, inc=1, device_id={"sec": peer}, device_id_type=MESH)

    @pl.when(has_upper)
    def _():
        pl.semaphore_signal(barrier, inc=1, device_id={"tile": tile - 1}, device_id_type=MESH)

    @pl.when(has_lower)
    def _():
        pl.semaphore_signal(barrier, inc=1, device_id={"tile": tile + 1}, device_id_type=MESH)

    rows = pl.ds(PAD, height)

    def load_field(cb):
        lanes = pl.ds(pl.multiple_of(cb * LANES, LANES), LANES)
        return pltpu.make_async_copy(disp.at[:, 0, :, lanes], f_a.at[:, cb + 1, rows, :], load_sem.at[cb])

    def load_spring(cb):
        lanes = pl.ds(pl.multiple_of(cb * LANES, LANES), LANES)
        return pltpu.make_async_copy(spring.at[0, :, lanes], spr.at[cb], spring_sem.at[cb])

    own_lists = [
        pltpu.make_async_copy(blocks.at[0], own_index, list_sem.at[0]),
        pltpu.make_async_copy(blocks.at[0], own_blocks, list_sem.at[1]),
        pltpu.make_async_copy(classes, own_class, list_sem.at[2]),
    ]
    for copy in own_lists:
        copy.start()

    def start_loads(cb, carry):
        load_field(cb).start()
        return carry

    lax.fori_loop(0, columns, start_loads, 0)

    def start_springs(cb, carry):
        load_spring(cb).start()
        return carry

    lax.fori_loop(0, columns, start_springs, 0)

    for field in (f_a, f_b):
        for cb in (0, columns + 1):
            field[:, cb] = jnp.zeros((fields, height + 2 * PAD, LANES), F32)
        field[:, :, 0:PAD] = jnp.zeros((fields, columns + 2, PAD, LANES), F32)
        field[:, :, PAD + height :] = jnp.zeros((fields, columns + 2, PAD, LANES), F32)

    pl.semaphore_wait(barrier, 2 + has_upper.astype(jnp.int32) + has_lower.astype(jnp.int32))

    list_copies = [
        pltpu.make_async_remote_copy(
            src_ref=src, dst_ref=dst, send_sem=list_send.at[i], recv_sem=list_recv.at[i],
            device_id={"sec": following}, device_id_type=MESH,
        )
        for i, (src, dst) in enumerate(((blocks.at[1], prev_blocks), (classes, prev_class)))
    ]
    for copy in list_copies:
        copy.start()

    def edge_copies(step):
        upward = pltpu.make_async_remote_copy(
            src_ref=edge_out.at[step, 0], dst_ref=edge_in.at[step, 1],
            send_sem=edge_send.at[step, 0], recv_sem=edge_recv.at[step, 1],
            device_id={"tile": tile - 1}, device_id_type=MESH,
        )
        downward = pltpu.make_async_remote_copy(
            src_ref=edge_out.at[step, 1], dst_ref=edge_in.at[step, 0],
            send_sem=edge_send.at[step, 1], recv_sem=edge_recv.at[step, 0],
            device_id={"tile": tile + 1}, device_id_type=MESH,
        )
        return upward, downward

    def row_copy(step, side, chunk):
        mine = side * matches + chunk * part
        theirs = (1 - side) * matches + chunk * part
        return pltpu.make_async_remote_copy(
            src_ref=sent.at[step, :, pl.ds(mine, part), :],
            dst_ref=received.at[step, :, pl.ds(theirs, part), :],
            send_sem=row_send.at[step, side, chunk],
            recv_sem=row_recv.at[step, 1 - side, chunk],
            device_id={"sec": (following, previous)[side]}, device_id_type=MESH,
        )

    def row_arrival(step, side, chunk):
        mine = side * matches + chunk * part
        return pltpu.make_async_remote_copy(
            src_ref=sent.at[step, :, pl.ds(mine, part), :],
            dst_ref=received.at[step, :, pl.ds(mine, part), :],
            send_sem=row_send.at[step, side, chunk],
            recv_sem=row_recv.at[step, side, chunk],
            device_id={"sec": (following, previous)[side]}, device_id_type=MESH,
        )

    def place(block):
        return block % columns, block // columns

    def gather_rows(index, first, count, base, put):
        def group(g, carry):
            at = pl.multiple_of(first + g * 8, 8)
            for j in range(8):
                cb, row = place(index[0, at + j])
                put(base + at + j, cb, row)
            return carry

        lax.fori_loop(0, count // 8, group, 0)

    def put_sent(field):
        def put(at, cb, row):
            for c in range(fields):
                sent[0, c, pl.ds(at, 1), :] = field[c, cb + 1, pl.ds(PAD + row, 1), :]
        return put

    def put_l(field):
        def put(at, cb, row):
            for c in range(fields):
                gathered_l[c, pl.ds(at, 1), :] = field[c, cb + 1, pl.ds(PAD + row, 1), :]
        return put

    def put_g(at, cb, row):
        gathered_g[pl.ds(at, 1), :] = g_ref[cb, pl.ds(row, 1), :]

    own_lists[0].wait()

    def wait_loads(cb, carry):
        load_field(cb).wait()
        return carry

    lax.fori_loop(0, columns, wait_loads, 0)
    for chunk in range(CHUNKS):
        gather_rows(own_index, chunk * part, part, 0, put_sent(f_a))
        row_copy(0, 0, chunk).start()
    for copy in list_copies:
        copy.wait_recv()
    to_scalar = pltpu.make_async_copy(prev_blocks, prev_index, list_sem.at[0])
    to_scalar.start()

    def send_edges(step, field):
        def one(cb, carry):
            for c in range(fields):
                at = pl.ds(c * columns + cb, 1)
                edge_out[step, 0, at, :] = field[c, cb + 1, PAD : PAD + 1, :]
                edge_out[step, 1, at, :] = field[c, cb + 1, PAD + height - 1 : PAD + height, :]
            return carry

        lax.fori_loop(0, columns, one, 0)
        upward, downward = edge_copies(step)

        @pl.when(has_upper)
        def _():
            upward.start()

        @pl.when(has_lower)
        def _():
            downward.start()

    to_scalar.wait()
    for chunk in range(CHUNKS):
        gather_rows(prev_index, chunk * part, part, matches, put_sent(f_a))
        row_copy(0, 1, chunk).start()
    send_edges(0, f_a)

    own_lists[1].wait()
    own_lists[2].wait()
    lane = lax.broadcasted_iota(jnp.int32, (STRIP, LANES), 1)
    block_rows = []
    for side, (index_ref, class_ref, alive) in enumerate(
        ((own_blocks, own_class, section < sections - 1), (prev_blocks, prev_class, section > 0))
    ):
        index = index_ref[...].astype(F32)
        kind = class_ref[...]
        stiff = jnp.zeros(kind.shape, F32)
        for level in range(table.shape[0]):
            stiff = jnp.where(kind == level, table[level], stiff)
        stiff = stiff * jnp.where(alive, 1.0, 0.0)
        half = pl.ds(side * matches, matches)
        block_cols[half, :] = jnp.transpose(jnp.broadcast_to(index, (LANES, matches)))
        cmat[half, :] = jnp.transpose(jnp.broadcast_to(stiff, (LANES, matches)))
        block_rows.append(index)

    def fill_pmat(g, carry):
        at = pl.ds(pl.multiple_of(g * STRIP, STRIP), STRIP)
        col = block_cols[at, :]
        for side in range(2):
            for j in range(matches // LANES):
                row = block_rows[side][:, j * LANES : (j + 1) * LANES]
                first = side * matches + j * LANES
                pmat[at, first : first + LANES] = jnp.where(col == row, 1.0, 0.0).astype(BF16)
        return carry

    lax.fori_loop(0, 2 * matches // STRIP, fill_pmat, 0)

    def fill_onehot(g, carry):
        cb, strip = g // (height // STRIP), g % (height // STRIP)
        first = pl.multiple_of(strip * STRIP, STRIP)
        row = first + lax.broadcasted_iota(jnp.int32, (STRIP, LANES), 0)
        block = (row * columns + cb).astype(F32)
        for side in range(2):
            for j in range(matches // LANES):
                wanted = block_rows[side][:, j * LANES : (j + 1) * LANES]
                at = side * matches + j * LANES
                onehot[cb, pl.ds(first, STRIP), at : at + LANES] = jnp.where(block == wanted, 1.0, 0.0).astype(BF16)
        return carry

    lax.fori_loop(0, columns * (height // STRIP), fill_onehot, 0)

    c_high, c_low = split(cmat[...])
    c_parts = jnp.concatenate([c_high, c_low], axis=1)

    def fill_gain(cb, carry):
        load_spring(cb).wait()
        sums = jnp.dot(onehot[cb], c_parts, preferred_element_type=F32)
        stiff = spr[cb]
        gain = 0.8 / (4.0 * stiff + (sums[:, :LANES] + sums[:, LANES:]))
        g_ref[cb] = gain
        a_ref[cb] = gain * stiff
        return carry

    lax.fori_loop(0, columns, fill_gain, 0)
    gather_rows(own_index, 0, matches, 0, put_g)
    gather_rows(prev_index, 0, matches, matches, put_g)

    def stencil(field, result):
        def one(cb, carry):
            for s in range(height // STRIP):
                top = PAD + s * STRIP
                at = pl.ds(top, STRIP)
                a = a_ref[cb, s * STRIP : (s + 1) * STRIP]
                for c in range(fields):
                    here = field[c, cb + 1, at]
                    west, east = field[c, cb, at], field[c, cb + 2, at]
                    north = field[c, cb + 1, pl.ds(top - 1, STRIP)]
                    south = field[c, cb + 1, pl.ds(top + 1, STRIP)]
                    west = pltpu.roll(jnp.where(lane == LANES - 1, west, here), 1, axis=1)
                    east = pltpu.roll(jnp.where(lane == 0, east, here), LANES - 1, axis=1)
                    lap = ((north + south) + (west + east)) - 4.0 * here
                    result[c, cb + 1, at] = here + a * lap
            return carry

        lax.fori_loop(0, columns, one, 0)

    def add_edge(step, which, result):
        row = (0, height - 1)[which]

        def one(cb, carry):
            a = a_ref[cb, row : row + 1, :]
            for c in range(fields):
                at = pl.ds(c * columns + cb, 1)
                result[c, cb + 1, PAD + row : PAD + row + 1, :] += a * edge_in[step, which, at, :]
            return carry

        lax.fori_loop(0, columns, one, 0)

    def add_edges(step, result):
        upward, downward = edge_copies(step)

        @pl.when(has_upper)
        def _():
            pltpu.make_async_remote_copy(
                src_ref=edge_out.at[step, 0], dst_ref=edge_in.at[step, 0],
                send_sem=edge_send.at[step, 0], recv_sem=edge_recv.at[step, 0],
                device_id={"tile": tile - 1}, device_id_type=MESH,
            ).wait_recv()
            add_edge(step, 0, result)
            upward.wait_send()

        @pl.when(has_lower)
        def _():
            pltpu.make_async_remote_copy(
                src_ref=edge_out.at[step, 1], dst_ref=edge_in.at[step, 1],
                send_sem=edge_send.at[step, 1], recv_sem=edge_recv.at[step, 1],
                device_id={"tile": tile + 1}, device_id_type=MESH,
            ).wait_recv()
            add_edge(step, 1, result)
            downward.wait_send()

    def update(cb, result):
        sums = jnp.dot(onehot[cb], t_high[...], preferred_element_type=F32)
        sums = sums + jnp.dot(onehot[cb], t_low[...], preferred_element_type=F32)
        gain = g_ref[cb]
        for c in range(fields):
            result[c, cb + 1, rows, :] += gain * sums[:, c * LANES : (c + 1) * LANES]

    def store(cb, result):
        lanes = pl.ds(pl.multiple_of(cb * LANES, LANES), LANES)
        return pltpu.make_async_copy(result.at[:, cb + 1, rows, :], out.at[:, 0, :, lanes], out_sem.at[cb])

    field, result = f_a, f_b
    for step in range(ITERS):
        last = step == ITERS - 1
        stencil(field, result)
        add_edges(step, result)
        if not last:
            gather_rows(own_index, 0, matches, 0, put_l(result))
            gather_rows(prev_index, 0, matches, matches, put_l(result))
        for side in range(2):
            for chunk in range(CHUNKS):
                row_arrival(step, side, chunk).wait_recv()
                at = pl.ds(side * matches + chunk * part, part)
                c = cmat[at, :]
                for f in range(fields):
                    lanes = slice(f * LANES, (f + 1) * LANES)
                    high, low = split(c * (received[step, f, at, :] - sent[step, f, at, :]))
                    t_high[at, lanes] = high
                    t_low[at, lanes] = low
        if not last:
            for chunk in range(CHUNKS):
                for side in range(2):
                    at = pl.ds(side * matches + chunk * part, part)
                    sums = jnp.dot(pmat[at, :], t_high[...], preferred_element_type=F32)
                    sums = sums + jnp.dot(pmat[at, :], t_low[...], preferred_element_type=F32)
                    gain = gathered_g[at, :]
                    for f in range(fields):
                        lanes = slice(f * LANES, (f + 1) * LANES)
                        sent[step + 1, f, at, :] = gathered_l[f, at, :] + gain * sums[:, lanes]
                    row_copy(step + 1, side, chunk).start()

            def full(cb, carry):
                update(cb, result)
                return carry

            lax.fori_loop(0, columns, full, 0)
            send_edges(step + 1, result)
        else:

            def finish(cb, carry):
                update(cb, result)
                store(cb, result).start()
                return carry

            lax.fori_loop(0, columns, finish, 0)
        field, result = result, field

    for copy in list_copies:
        copy.wait_send()
    for step in range(ITERS):
        for side in range(2):
            for chunk in range(CHUNKS):
                row_copy(step, side, chunk).wait_send()

    def drain(cb, carry):
        store(cb, field).wait()
        return carry

    lax.fori_loop(0, columns, drain, 0)


def on_device(displacement, spring, stiff_table, match_blocks, match_class):
    fields, _, height, breadth = displacement.shape
    columns = breadth // LANES
    matches = match_class.shape[1]
    both = 2 * matches
    width = fields * LANES
    vmem, smem, dma = pltpu.VMEM, pltpu.SMEM, pltpu.SemaphoreType.DMA
    padded = (fields, columns + 2, height + 2 * PAD, LANES)
    anywhere = pl.BlockSpec(memory_space=pl.ANY)
    return pl.pallas_call(
        kernel,
        out_shape=jax.ShapeDtypeStruct(displacement.shape, F32),
        in_specs=[anywhere, anywhere, pl.BlockSpec(memory_space=smem), anywhere, anywhere],
        out_specs=anywhere,
        scratch_shapes=[
            vmem(padded, F32), vmem(padded, F32),
            vmem((columns, height, LANES), F32),
            vmem((columns, height, LANES), F32),
            vmem((columns, height, LANES), F32),
            vmem((columns, height, both), BF16),
            vmem((both, both), BF16),
            smem((1, matches), jnp.int32), smem((1, matches), jnp.int32),
            vmem((1, matches), jnp.int32), vmem((1, matches), jnp.int32),
            vmem((1, matches), jnp.int32), vmem((1, matches), jnp.int32),
            vmem((both, LANES), F32), vmem((both, LANES), F32), vmem((both, LANES), F32),
            vmem((fields, both, LANES), F32),
            vmem((ITERS, fields, both, LANES), F32), vmem((ITERS, fields, both, LANES), F32),
            vmem((both, width), BF16), vmem((both, width), BF16),
            vmem((ITERS, 2, fields * columns, LANES), F32), vmem((ITERS, 2, fields * columns, LANES), F32),
            dma((columns,)), dma((columns,)), dma((3,)), dma((2,)), dma((2,)),
            dma((ITERS, 2, CHUNKS)), dma((ITERS, 2, CHUNKS)), dma((ITERS, 2)), dma((ITERS, 2)),
            dma((columns,)),
        ],
        compiler_params=pltpu.CompilerParams(
            collective_id=0, has_side_effects=True, vmem_limit_bytes=48 * 1024 * 1024
        ),
    )(displacement, spring, stiff_table, match_blocks, match_class)


def solution(mesh):
    placed = (
        P(None, "sec", "tile", None),
        P("sec", "tile", None),
        P(),
        P(None, "sec", "tile"),
        P("sec", "tile"),
    )
    return jax.shard_map(
        on_device,
        mesh=mesh,
        in_specs=placed,
        out_specs=P(None, "sec", "tile", None),
        check_vma=False,
    )
```

time: 492 us -> 69.8 us (0.14)
  the two profiles are of different devices: /device:TPU:97 before, /device:TPU:1 now
where the time goes in v1:
time: 69.8 us; the launch traced here: 69.6 us
  Pallas kernels  61.3 us (88%)
  local copies, waits for them, and re-layouts  8.3 us (12%)
    pallas_call x1, Pallas kernels, on_device(): pl.pallas_call(kernel, out_shape=jax.ShapeDtypeStruct(displacement.shape,...  61.3 us
    unnamed x9, local copies, waits for them, and re-layouts  8.3 us

profile of v1, /device:TPU:1, one launch (start us, length us, event | category | flops | bytes accessed | tf_op | source)
XLA Modules:
  0.0 69.6 jit_solution(15517565061732248943)
XLA Ops:
  0.0 0.0 copy-start
  0.0 1.6 %copy-done = f32[1,256,2048]{2,1,0:T(8,128)S(1)} copy-done((f32[1,256,2048]{2,1,0:T(8,128)S(1)}, f32[1,256,2048]{2,1,0:T(8,128)}, u32[]{:S(2)}) %copy-start) | copy-done | bytes 2097176
  1.6 0.0 copy-start.1
  1.6 0.7 copy-done.1
  2.3 0.0 copy-start.2
  2.3 0.7 copy-done.2
  3.0 0.0 copy-start.3
  3.0 0.7 copy-done.3
  3.6 61.3 %shard_map.55 = f32[2,1,256,2048]{3,2,1,0:T(8,128)} custom-call(f32[2,1,256,2048]{3,2,1,0:T(8,128)} %disp.1, f32[1,256,2048]{2,1,0:T(8,128)S(1)} %copy-done, f32[8]{0:T(128)S(1)} %copy-done.3, s32[2,1,256]{2,1,0:T(1,128)S(1)} %copy-done.1, s32[1,256]{1,0:T(1,128)S(1)} %copy-done.2), custom_call_target="tpu_custom_call" | custom-call | tf_op jit(solution)/shard_map/pallas_call | solution.py:400
  64.9 4.7 %copy.7 = f32[2,1,256,2048]{3,2,1,0:T(8,128)} copy(f32[2,1,256,2048]{3,2,1,0:T(8,128)} %shard_map.55) | data formatting | bytes 8388608
Async XLA Ops:
  0.0 1.6 %copy-start = (f32[1,256,2048]{2,1,0:T(8,128)S(1)}, f32[1,256,2048]{2,1,0:T(8,128)}, u32[]{:S(2)}) copy-start(f32[1,256,2048]{2,1,0:T(8,128)} %spring.1) | copy-start | bytes 6291460
  1.6 0.7 copy-start.1
  2.3 0.7 copy-start.2
  3.0 0.7 copy-start.3

commit v2 on v0

v2 whole, which is shorter than its diff:
```python
import jax
import jax.numpy as jnp
from jax import lax
from jax.experimental import pallas as pl
from jax.experimental.pallas import tpu as pltpu
from jax.sharding import PartitionSpec as P

ITERS = 3
LANES = 128
PAD = 8
CHUNKS = 2
STRIP = 64
MESH = pl.DeviceIdType.MESH
F32 = jnp.float32
BF16 = jnp.bfloat16
I32 = jnp.int32


def split(value):
    high = value.astype(BF16)
    return high, (value - high.astype(F32)).astype(BF16)


def loop(count, body):
    def step(i, carry):
        body(i)
        return carry

    lax.fori_loop(0, count, step, 0)


def relax(
    disp, spring, table_hbm, blocks, classes,
    f_b, last_rows, index,
    f_a, spr, a_ref, g_ref, onehot, pmat,
    table, raw_blocks, lists_out, lists_in, lists_own,
    cmat, c_parts, block_cols, gathered_g, gathered_l, sent, received, terms,
    edge_out, edge_in,
    load_sem, spring_sem, list_sem, list_send, list_recv,
    row_send, row_recv, edge_send, edge_recv,
):
    fields, _, height, breadth = disp.shape
    columns = breadth // LANES
    stride = height + PAD
    matches = classes.shape[1]
    both = 2 * matches
    part = matches // CHUNKS
    section, sections = lax.axis_index("sec"), lax.axis_size("sec")
    tile, tiles = lax.axis_index("tile"), lax.axis_size("tile")
    has_next, has_prev = section < sections - 1, section > 0
    has_upper, has_lower = tile > 0, tile < tiles - 1
    neighbours = (
        (has_next, {"sec": section + 1}),
        (has_prev, {"sec": section - 1}),
        (has_upper, {"tile": tile - 1}),
        (has_lower, {"tile": tile + 1}),
    )

    def first_row(cb):
        return pl.multiple_of((cb + 1) * stride + PAD, PAD)

    def lanes_of(cb):
        return pl.ds(pl.multiple_of(cb * LANES, LANES), LANES)

    barrier = pltpu.get_barrier_semaphore()
    for there, peer in neighbours:

        @pl.when(there)
        def _(peer=peer):
            pl.semaphore_signal(barrier, inc=1, device_id=peer, device_id_type=MESH)

    own_copies = [
        pltpu.make_async_copy(blocks, raw_blocks, list_sem.at[0]),
        pltpu.make_async_copy(classes, lists_own.at[1], list_sem.at[1]),
        pltpu.make_async_copy(table_hbm, table, list_sem.at[2]),
    ]
    for copy in own_copies:
        copy.start()

    def load_field(cb):
        return pltpu.make_async_copy(
            disp.at[:, 0, :, lanes_of(cb)], f_a.at[:, pl.ds(first_row(cb), height), :], load_sem.at[cb]
        )

    def load_spring(cb):
        return pltpu.make_async_copy(spring.at[0, :, lanes_of(cb)], spr.at[cb], spring_sem.at[cb])

    loop(columns, lambda cb: load_field(cb).start())
    loop(columns, lambda cb: load_spring(cb).start())

    zero_block = jnp.zeros((fields, stride, LANES), F32)
    zero_pad = jnp.zeros((fields, PAD, LANES), F32)
    for field in (f_a, f_b):
        field[:, 0:stride, :] = zero_block
        field[:, (columns + 1) * stride + PAD :, :] = zero_block
        loop(columns, lambda cb: field.__setitem__((slice(None), pl.ds(first_row(cb) + height, PAD), slice(None)), zero_pad))
    for there, side in ((has_next, 0), (has_prev, 1)):

        @pl.when(jnp.logical_not(there))
        def _(side=side):
            received[:, :, side * matches : (side + 1) * matches, :] = jnp.zeros((ITERS, fields, matches, LANES), F32)

    for copy in own_copies:
        copy.wait()

    def address(block):
        return (block % columns + 1) * stride + PAD + block // columns

    lists_own[0] = address(raw_blocks[0])
    lists_out[0] = address(raw_blocks[1])
    lists_out[1] = lists_own[1]
    own_scalar = pltpu.make_async_copy(lists_own.at[0], index.at[0], list_sem.at[0])
    own_scalar.start()

    pl.semaphore_wait(barrier, sum(there.astype(I32) for there, _ in neighbours))

    list_copy = pltpu.make_async_remote_copy(
        src_ref=lists_out, dst_ref=lists_in, send_sem=list_send, recv_sem=list_recv,
        device_id={"sec": section + 1}, device_id_type=MESH,
    )
    pl.when(has_next)(list_copy.start)

    def edge_copy(step, way):
        return pltpu.make_async_remote_copy(
            src_ref=edge_out.at[step, way], dst_ref=edge_in.at[step, 1 - way],
            send_sem=edge_send.at[step, way], recv_sem=edge_recv.at[step, 1 - way],
            device_id=neighbours[2 + way][1], device_id_type=MESH,
        )

    def edge_arrival(step, way):
        return pltpu.make_async_remote_copy(
            src_ref=edge_out.at[step, way], dst_ref=edge_in.at[step, way],
            send_sem=edge_send.at[step, way], recv_sem=edge_recv.at[step, way],
            device_id=neighbours[2 + way][1], device_id_type=MESH,
        )

    def row_copy(step, side, chunk, arrival=False):
        mine = side * matches + chunk * part
        theirs = mine if arrival else (1 - side) * matches + chunk * part
        return pltpu.make_async_remote_copy(
            src_ref=sent.at[step, :, pl.ds(mine, part), :],
            dst_ref=received.at[step, :, pl.ds(theirs, part), :],
            send_sem=row_send.at[step, side, chunk],
            recv_sem=row_recv.at[step, side if arrival else 1 - side, chunk],
            device_id=neighbours[side][1], device_id_type=MESH,
        )

    def send_rows(step, side, chunk):
        pl.when(neighbours[side][0])(row_copy(step, side, chunk).start)

    def gather(side, first, count, source, put):
        def group(g):
            at = pl.multiple_of(first + g * 16, 16)
            rows = [source(index[side, 0, at + j]) for j in range(16)]
            for j in range(16):
                put(side * matches + at + j, rows[j])

        loop(count // 16, group)

    def rows_of(ref):
        return lambda at: ref[:, pl.ds(at, 1), :]

    def put_sent(at, row):
        sent[0, :, pl.ds(at, 1), :] = row

    def put_l(at, row):
        gathered_l[:, pl.ds(at, 1), :] = row

    def put_g(at, row):
        gathered_g[pl.ds(at, 1), :] = row

    own_scalar.wait()
    loop(columns, lambda cb: load_field(cb).wait())
    for chunk in range(CHUNKS):
        gather(0, chunk * part, part, rows_of(f_a), put_sent)
        send_rows(0, 0, chunk)

    def send_edges(step, field):
        def one(cb):
            top = first_row(cb)
            for c in range(fields):
                at = pl.ds(c * columns + cb, 1)
                edge_out[step, 0, at, :] = field[c, pl.ds(top, 1), :]
                edge_out[step, 1, at, :] = field[c, pl.ds(top + height - 1, 1), :]

        loop(columns, one)
        for way in range(2):
            pl.when(neighbours[2 + way][0])(edge_copy(step, way).start)

    send_edges(0, f_a)

    def stiffness(lists, alive):
        kind = lists[1]
        stiff = jnp.zeros(kind.shape, F32)
        for level in range(table.shape[0]):
            stiff = jnp.where(kind == level, table[level], stiff)
        return stiff * jnp.where(alive, 1.0, 0.0)

    def fill_side(side, lists, alive):
        half = pl.ds(side * matches, matches)
        wanted = lists[0]
        stiff = jnp.transpose(jnp.broadcast_to(stiffness(lists, alive), (LANES, matches)))
        cmat[half, :] = stiff
        high, low = split(stiff)
        c_parts[half, 0:LANES] = high
        c_parts[half, LANES:] = low
        block_cols[half, :] = jnp.transpose(jnp.broadcast_to(wanted.astype(F32), (LANES, matches)))

        def one(g):
            cb, strip = g // (height // STRIP), g % (height // STRIP)
            row = first_row(cb) + strip * STRIP + lax.broadcasted_iota(I32, (STRIP, LANES), 0)
            at = pl.ds(pl.multiple_of(g * STRIP, STRIP), STRIP)
            for j in range(matches // LANES):
                hit = row == wanted[:, j * LANES : (j + 1) * LANES]
                first = side * matches + j * LANES
                onehot[at, first : first + LANES] = jnp.where(hit, 1.0, 0.0).astype(BF16)

        loop(columns * (height // STRIP), one)

    fill_side(0, lists_own, has_next)

    @pl.when(has_prev)
    def _():
        list_copy.wait_recv()

    @pl.when(jnp.logical_not(has_prev))
    def _():
        lists_in[...] = lists_out[...]

    prev_scalar = pltpu.make_async_copy(lists_in.at[0], index.at[1], list_sem.at[0])
    prev_scalar.start()
    prev_scalar.wait()
    for chunk in range(CHUNKS):
        gather(1, chunk * part, part, rows_of(f_a), put_sent)
        send_rows(0, 1, chunk)
    fill_side(1, lists_in, has_prev)

    def fill_pmat(g):
        at = pl.ds(pl.multiple_of(g * STRIP, STRIP), STRIP)
        col = block_cols[at, :]
        for side, lists in enumerate((lists_own, lists_in)):
            row = lists[0].astype(F32)
            for j in range(matches // LANES):
                hit = jnp.where(col == row[:, j * LANES : (j + 1) * LANES], 1.0, 0.0).astype(BF16)
                first = side * matches + j * LANES
                pmat[at, first : first + LANES] = hit
                pmat[at, both + first : both + first + LANES] = hit

    loop(both // STRIP, fill_pmat)

    def fill_gain(p):
        for q in range(2):
            cb = p * 2 + q
            load_spring(cb).wait()
            at = pl.ds(pl.multiple_of(cb * height, height), height)
            sums = jnp.dot(onehot[at, :], c_parts[...], preferred_element_type=F32)
            stiff = spr[cb]
            gain = 0.8 / (4.0 * stiff + (sums[:, :LANES] + sums[:, LANES:]))
            at = pl.ds(first_row(cb), height)
            g_ref[at, :] = gain
            a_ref[at, :] = gain * stiff

    loop(columns // 2, fill_gain)
    for side in range(2):
        gather(side, 0, matches, lambda at: g_ref[pl.ds(at, 1), :], put_g)

    lane = lax.broadcasted_iota(I32, (STRIP, LANES), 1)

    def stencil(field, result):
        def one(cb):
            for s in range(height // STRIP):
                top = first_row(cb) + s * STRIP
                at = pl.ds(top, STRIP)
                a = a_ref[at, :]
                for c in range(fields):
                    here = field[c, at, :]
                    west, east = field[c, pl.ds(top - stride, STRIP), :], field[c, pl.ds(top + stride, STRIP), :]
                    north, south = field[c, pl.ds(top - 1, STRIP), :], field[c, pl.ds(top + 1, STRIP), :]
                    west = pltpu.roll(jnp.where(lane == LANES - 1, west, here), 1, axis=1)
                    east = pltpu.roll(jnp.where(lane == 0, east, here), LANES - 1, axis=1)
                    result[c, at, :] = here + a * (((north + south) + (west + east)) - 4.0 * here)

        loop(columns, one)

    def add_edges(step, result):
        for way in range(2):

            @pl.when(neighbours[2 + way][0])
            def _(way=way):
                edge_arrival(step, way).wait_recv()

                def one(cb):
                    at = pl.ds(first_row(cb) + way * (height - 1), 1)
                    a = a_ref[at, :]
                    for c in range(fields):
                        result[c, at, :] += a * edge_in[step, way, pl.ds(c * columns + cb, 1), :]

                loop(columns, one)

    group = 4

    def update(g, result):
        at = pl.ds(pl.multiple_of(g * group * height, group * height), group * height)
        sums = jnp.dot(onehot[at, :], terms[0:both, :], preferred_element_type=F32)
        sums = sums + jnp.dot(onehot[at, :], terms[both:, :], preferred_element_type=F32)
        for w in range(group):
            at = pl.ds(first_row(g * group + w), height)
            gain = g_ref[at, :]
            for c in range(fields):
                result[c, at, :] += gain * sums[w * height : (w + 1) * height, c * LANES : (c + 1) * LANES]

    field, result = f_a, f_b
    for step in range(ITERS):
        last = step == ITERS - 1
        stencil(field, result)
        add_edges(step, result)
        for side in range(2):
            gather(side, 0, matches, rows_of(result), put_l)
        for chunk in range(CHUNKS):
            for side in range(2):
                pl.when(neighbours[side][0])(row_copy(step, side, chunk, True).wait_recv)
                first = side * matches + chunk * part
                at = pl.ds(first, part)
                c = cmat[at, :]
                for f in range(fields):
                    lanes = slice(f * LANES, (f + 1) * LANES)
                    high, low = split(c * (received[step, f, at, :] - sent[step, f, at, :]))
                    terms[first : first + part, lanes] = high
                    terms[both + first : both + first + part, lanes] = low
        for chunk in range(CHUNKS):
            for side in range(2):
                at = pl.ds(side * matches + chunk * part, part)
                sums = jnp.dot(pmat[at, :], terms[...], preferred_element_type=F32)
                gain = gathered_g[at, :]
                for f in range(fields):
                    row = gathered_l[f, at, :] + gain * sums[:, f * LANES : (f + 1) * LANES]
                    if last:
                        last_rows[f, at, :] = row
                    else:
                        sent[step + 1, f, at, :] = row
                if not last:
                    send_rows(step + 1, side, chunk)
        if not last:
            loop(columns // group, lambda g: update(g, result))
            send_edges(step + 1, result)
        field, result = result, field

    pl.when(has_next)(list_copy.wait_send)
    for step in range(ITERS):
        for way in range(2):
            pl.when(neighbours[2 + way][0])(edge_copy(step, way).wait_send)
        for side in range(2):
            for chunk in range(CHUNKS):
                pl.when(neighbours[side][0])(row_copy(step, side, chunk).wait_send)


def finish(base, rows, index, out, field, scalar, index_sem, out_sem):
    fields, _, height, breadth = out.shape
    columns = breadth // LANES
    stride = height + PAD
    matches = index.shape[2]

    def group(side):
        def one(g):
            at = pl.multiple_of(g * 16, 16)
            got = [rows[:, pl.ds(side * matches + at + j, 1), :] for j in range(16)]
            for j in range(16):
                field[:, pl.ds(index[side, 0, at + j], 1), :] = got[j]

        return one

    for side in range(2):
        loop(matches // 16, group(side))

    def store(cb):
        top = pl.multiple_of((cb + 1) * stride + PAD, PAD)
        lanes = pl.ds(pl.multiple_of(cb * LANES, LANES), LANES)
        return pltpu.make_async_copy(field.at[:, pl.ds(top, height), :], out.at[:, 0, :, lanes], out_sem.at[cb])

    loop(columns, lambda cb: store(cb).start())
    loop(columns, lambda cb: store(cb).wait())


def on_device(displacement, spring, stiff_table, match_blocks, match_class):
    fields, _, height, breadth = displacement.shape
    columns = breadth // LANES
    matches = match_class.shape[1]
    both = 2 * matches
    width = fields * LANES
    vmem, smem, dma = pltpu.VMEM, pltpu.SMEM, pltpu.SemaphoreType.DMA
    total = (columns + 2) * (height + PAD) + PAD
    padded = (fields, total, LANES)
    anywhere = pl.BlockSpec(memory_space=pl.ANY)
    in_vmem, in_smem = pl.BlockSpec(memory_space=vmem), pl.BlockSpec(memory_space=smem)
    arguments = [
        pltpu.with_memory_space_constraint(x, pltpu.HBM)
        for x in (displacement, spring, stiff_table, match_blocks, match_class)
    ]
    base, rows, index = pl.pallas_call(
        relax,
        out_shape=(vmem(padded, F32), vmem((fields, both, LANES), F32), smem((2, 1, matches), I32)),
        in_specs=[anywhere] * 5,
        out_specs=(in_vmem, in_vmem, in_smem),
        scratch_shapes=[
            vmem(padded, F32),
            vmem((columns, height, LANES), F32),
            vmem((total, LANES), F32), vmem((total, LANES), F32),
            vmem((columns * height, both), BF16),
            vmem((both, 2 * both), BF16),
            smem(stiff_table.shape, F32),
            vmem((2, 1, matches), I32), vmem((2, 1, matches), I32), vmem((2, 1, matches), I32), vmem((2, 1, matches), I32),
            vmem((both, LANES), F32), vmem((both, width), BF16), vmem((both, LANES), F32), vmem((both, LANES), F32),
            vmem((fields, both, LANES), F32),
            vmem((ITERS, fields, both, LANES), F32), vmem((ITERS, fields, both, LANES), F32),
            vmem((2 * both, width), BF16),
            vmem((ITERS, 2, fields * columns, LANES), F32), vmem((ITERS, 2, fields * columns, LANES), F32),
            dma((columns,)), dma((columns,)), dma((3,)), dma, dma,
            dma((ITERS, 2, CHUNKS)), dma((ITERS, 2, CHUNKS)), dma((ITERS, 2)), dma((ITERS, 2)),
        ],
        compiler_params=pltpu.CompilerParams(
            collective_id=0, has_side_effects=True, vmem_limit_bytes=48 * 1024 * 1024
        ),
    )(*arguments)
    relaxed, _ = pl.pallas_call(
        finish,
        out_shape=(jax.ShapeDtypeStruct(displacement.shape, F32), vmem(padded, F32)),
        in_specs=[in_vmem, in_vmem, in_smem],
        out_specs=(anywhere, in_vmem),
        scratch_shapes=[smem((2, 1, matches), I32), dma, dma((columns,))],
        input_output_aliases={0: 1},
        compiler_params=pltpu.CompilerParams(vmem_limit_bytes=24 * 1024 * 1024),
    )(base, rows, index)
    return relaxed


def solution(mesh):
    placed = (
        P(None, "sec", "tile", None),
        P("sec", "tile", None),
        P(),
        P(None, "sec", "tile"),
        P("sec", "tile"),
    )
    return jax.shard_map(
        on_device,
        mesh=mesh,
        in_specs=placed,
        out_specs=P(None, "sec", "tile", None),
        check_vma=False,
    )
```

time: 492 us -> 46 us (0.09)
  the two profiles are of different devices: /device:TPU:97 before, /device:TPU:8 now
where the time goes in v2:
time: 46 us; the launch traced here: 45.4 us
  Pallas kernels  45.4 us (99%)
    pallas_call x1, Pallas kernels, on_device(): pl.pallas_call(relax, out_shape=(vmem(padded, F32), vmem((fields, both, L...  42.3 us
    pallas_call x1, Pallas kernels, on_device(): pl.pallas_call(finish, out_shape=(jax.ShapeDtypeStruct(displacement.shape...  3.07 us

profile of v2, /device:TPU:8, one launch (start us, length us, event | category | flops | bytes accessed | tf_op | source)
XLA Modules:
  0.0 45.4 jit_solution(10229560336395719978)
XLA Ops:
  0.0 42.3 %shard_map.55 = (f32[2,4760,128]{2,1,0:T(8,128)S(1)}, f32[2,512,128]{2,1,0:T(8,128)S(1)}, s32[2,1,256]{2,1,0:T(1,128)S(4)}) custom-call(f32[2,1,256,2048]{3,2,1,0:T(8,128)} %disp.1, f32[1,256,2048]{2,1,0:T(8,128)} %spring.1, f32[8]{0:T(128)} %table_hbm.1, s32[2,1,256]{2,1,0:T(1,128)} %blocks.1, s32[1,256]{1,0:T(1,128)} %classes.1), custom_call_target="tpu_custom_call" | custom-call | tf_op jit(solution)/shard_map/pallas_call | solution.py:399
  42.4 3.1 %shard_map.56 = (f32[2,1,256,2048]{3,2,1,0:T(8,128)}, f32[2,4760,128]{2,1,0:T(8,128)S(1)}) custom-call(f32[2,4760,128]{2,1,0:T(8,128)S(1)} %get-tuple-element.9.base, f32[2,512,128]{2,1,0:T(8,128)S(1)} %get-tuple-element.10.rows, s32[2,1,256]{2,1,0:T(1,128)S(4)} %get-tuple-element.11.index), custom_call_target="tpu_custom_call", output_to_operand_aliasing={{1}: (0, {})} | custom-call | tf_op jit(solution)/shard_map/pallas_call | solution.py:424

commit v3 on v2

--- a/solution.py
+++ b/solution.py
@@ -9,6 +9,8 @@
 LANES = 128
 PAD = 8
 CHUNKS = 2
+LEFT = 2
+GROUP = 4
 STRIP = 64
 MESH = pl.DeviceIdType.MESH
 F32 = jnp.float32
@@ -34,7 +36,7 @@
     f_b, last_rows, index,
     f_a, spr, a_ref, g_ref, onehot, pmat,
     table, raw_blocks, lists_out, lists_in, lists_own,
-    cmat, c_parts, block_cols, gathered_g, gathered_l, sent, received, terms,
+    cmat, c_parts, block_cols, edge_hot, edge_g, partial, gathered_g, gathered_l, sent, received, terms,
     edge_out, edge_in,
     load_sem, spring_sem, list_sem, list_send, list_recv,
     row_send, row_recv, edge_send, edge_recv,
@@ -57,7 +59,7 @@
     )
 
     def first_row(cb):
-        return pl.multiple_of((cb + 1) * stride + PAD, PAD)
+        return pl.multiple_of((cb + LEFT) * stride + PAD, PAD)
 
     def lanes_of(cb):
         return pl.ds(pl.multiple_of(cb * LANES, LANES), LANES)
@@ -91,9 +93,13 @@
     zero_block = jnp.zeros((fields, stride, LANES), F32)
     zero_pad = jnp.zeros((fields, PAD, LANES), F32)
     for field in (f_a, f_b):
-        field[:, 0:stride, :] = zero_block
-        field[:, (columns + 1) * stride + PAD :, :] = zero_block
+        for cb in range(LEFT):
+            field[:, cb * stride : (cb + 1) * stride, :] = zero_block
+        field[:, (columns + LEFT) * stride + PAD :, :] = zero_block
+        field[:, LEFT * stride : LEFT * stride + PAD, :] = zero_pad
         loop(columns, lambda cb: field.__setitem__((slice(None), pl.ds(first_row(cb) + height, PAD), slice(None)), zero_pad))
+    for cb in range(LEFT):
+        a_ref[cb * stride : (cb + 1) * stride, :] = zero_block[0]
     for there, side in ((has_next, 0), (has_prev, 1)):
 
         @pl.when(jnp.logical_not(there))
@@ -104,7 +110,7 @@
         copy.wait()
 
     def address(block):
-        return (block % columns + 1) * stride + PAD + block // columns
+        return (block % columns + LEFT) * stride + PAD + block // columns
 
     lists_own[0] = address(raw_blocks[0])
     lists_out[0] = address(raw_blocks[1])
@@ -175,19 +181,23 @@
         gather(0, chunk * part, part, rows_of(f_a), put_sent)
         send_rows(0, 0, chunk)
 
-    def send_edges(step, field):
-        def one(cb):
-            top = first_row(cb)
-            for c in range(fields):
-                at = pl.ds(c * columns + cb, 1)
-                edge_out[step, 0, at, :] = field[c, pl.ds(top, 1), :]
-                edge_out[step, 1, at, :] = field[c, pl.ds(top + height - 1, 1), :]
-
-        loop(columns, one)
+    def send_edges(step):
         for way in range(2):
             pl.when(neighbours[2 + way][0])(edge_copy(step, way).start)
 
-    send_edges(0, f_a)
+    def each_edge(put):
+        def one(cb):
+            for way in range(2):
+                put(way, cb, first_row(cb) + way * (height - 1))
+
+        loop(columns, one)
+
+    def first_edge(way, cb, row):
+        for c in range(fields):
+            edge_out[0, way, pl.ds(c * columns + cb, 1), :] = f_a[c, pl.ds(row, 1), :]
+
+    each_edge(first_edge)
+    send_edges(0)
 
     def stiffness(lists, alive):
         kind = lists[1]
@@ -196,26 +206,37 @@
             stiff = jnp.where(kind == level, table[level], stiff)
         return stiff * jnp.where(alive, 1.0, 0.0)
 
+    def place(side, j):
+        first = j * LANES // part * 2 * part + side * part + j * LANES % part
+        return slice(first, first + LANES)
+
     def fill_side(side, lists, alive):
         half = pl.ds(side * matches, matches)
         wanted = lists[0]
         stiff = jnp.transpose(jnp.broadcast_to(stiffness(lists, alive), (LANES, matches)))
         cmat[half, :] = stiff
         high, low = split(stiff)
-        c_parts[half, 0:LANES] = high
-        c_parts[half, LANES:] = low
+        for j in range(matches // LANES):
+            from_rows = slice(j * LANES, (j + 1) * LANES)
+            c_parts[place(side, j), 0:LANES] = high[from_rows]
+            c_parts[place(side, j), LANES:] = low[from_rows]
         block_cols[half, :] = jnp.transpose(jnp.broadcast_to(wanted.astype(F32), (LANES, matches)))
 
-        def one(g):
-            cb, strip = g // (height // STRIP), g % (height // STRIP)
-            row = first_row(cb) + strip * STRIP + lax.broadcasted_iota(I32, (STRIP, LANES), 0)
-            at = pl.ds(pl.multiple_of(g * STRIP, STRIP), STRIP)
+        def hits(row, j):
+            hit = row == wanted[:, j * LANES : (j + 1) * LANES]
+            return jnp.where(hit, 1.0, 0.0).astype(BF16)
+
+        def one(cb):
+            row = first_row(cb) + lax.broadcasted_iota(I32, (height, LANES), 0)
+            at = pl.ds(pl.multiple_of(cb * height, height), height)
             for j in range(matches // LANES):
-                hit = row == wanted[:, j * LANES : (j + 1) * LANES]
-                first = side * matches + j * LANES
-                onehot[at, first : first + LANES] = jnp.where(hit, 1.0, 0.0).astype(BF16)
-
-        loop(columns * (height // STRIP), one)
+                onehot[at, place(side, j)] = hits(row, j)
+
+        loop(columns, one)
+        order = lax.broadcasted_iota(I32, (2 * columns, LANES), 0)
+        row = (order % columns + LEFT) * stride + PAD + order // columns * (height - 1)
+        for j in range(matches // LANES):
+            edge_hot[:, place(side, j)] = hits(row, j)
 
     fill_side(0, lists_own, has_next)
 
@@ -242,45 +263,36 @@
             row = lists[0].astype(F32)
             for j in range(matches // LANES):
                 hit = jnp.where(col == row[:, j * LANES : (j + 1) * LANES], 1.0, 0.0).astype(BF16)
-                first = side * matches + j * LANES
-                pmat[at, first : first + LANES] = hit
-                pmat[at, both + first : both + first + LANES] = hit
+                pmat[at, place(side, j)] = hit
 
     loop(both // STRIP, fill_pmat)
 
-    def fill_gain(p):
-        for q in range(2):
-            cb = p * 2 + q
-            load_spring(cb).wait()
-            at = pl.ds(pl.multiple_of(cb * height, height), height)
-            sums = jnp.dot(onehot[at, :], c_parts[...], preferred_element_type=F32)
+    def gains(g):
+        at = pl.ds(pl.multiple_of(g * GROUP * height, GROUP * height), GROUP * height)
+        sums = jnp.dot(onehot[at, :], c_parts[...], preferred_element_type=F32)
+        for w in range(GROUP):
+            cb = g * GROUP + w
+            here = sums[w * height : (w + 1) * height]
             stiff = spr[cb]
-            gain = 0.8 / (4.0 * stiff + (sums[:, :LANES] + sums[:, LANES:]))
+            gain = 0.8 / (4.0 * stiff + (here[:, :LANES] + here[:, LANES:]))
             at = pl.ds(first_row(cb), height)
             g_ref[at, :] = gain
             a_ref[at, :] = gain * stiff
 
-    loop(columns // 2, fill_gain)
-    for side in range(2):
-        gather(side, 0, matches, lambda at: g_ref[pl.ds(at, 1), :], put_g)
-
     lane = lax.broadcasted_iota(I32, (STRIP, LANES), 1)
 
-    def stencil(field, result):
-        def one(cb):
-            for s in range(height // STRIP):
-                top = first_row(cb) + s * STRIP
-                at = pl.ds(top, STRIP)
-                a = a_ref[at, :]
-                for c in range(fields):
-                    here = field[c, at, :]
-                    west, east = field[c, pl.ds(top - stride, STRIP), :], field[c, pl.ds(top + stride, STRIP), :]
-                    north, south = field[c, pl.ds(top - 1, STRIP), :], field[c, pl.ds(top + 1, STRIP), :]
-                    west = pltpu.roll(jnp.where(lane == LANES - 1, west, here), 1, axis=1)
-                    east = pltpu.roll(jnp.where(lane == 0, east, here), LANES - 1, axis=1)
-                    result[c, at, :] = here + a * (((north + south) + (west + east)) - 4.0 * here)
-
-        loop(columns, one)
+    def stencil(cb, field, result):
+        for s in range(height // STRIP):
+            top = first_row(cb) + s * STRIP
+            at = pl.ds(top, STRIP)
+            a = a_ref[at, :]
+            for c in range(fields):
+                here = field[c, at, :]
+                west, east = field[c, pl.ds(top - stride, STRIP), :], field[c, pl.ds(top + stride, STRIP), :]
+                north, south = field[c, pl.ds(top - 1, STRIP), :], field[c, pl.ds(top + 1, STRIP), :]
+                west = pltpu.roll(jnp.where(lane == LANES - 1, west, here), 1, axis=1)
+                east = pltpu.roll(jnp.where(lane == 0, east, here), LANES - 1, axis=1)
+                result[c, at, :] = here + a * (((north + south) + (west + east)) - 4.0 * here)
 
     def add_edges(step, result):
         for way in range(2):
@@ -297,52 +309,103 @@
 
                 loop(columns, one)
 
-    group = 4
-
-    def update(g, result):
-        at = pl.ds(pl.multiple_of(g * group * height, group * height), group * height)
+    def update(g, field):
+        at = pl.ds(pl.multiple_of(g * GROUP * height, GROUP * height), GROUP * height)
         sums = jnp.dot(onehot[at, :], terms[0:both, :], preferred_element_type=F32)
         sums = sums + jnp.dot(onehot[at, :], terms[both:, :], preferred_element_type=F32)
-        for w in range(group):
-            at = pl.ds(first_row(g * group + w), height)
+        for w in range(GROUP):
+            at = pl.ds(first_row(g * GROUP + w), height)
             gain = g_ref[at, :]
             for c in range(fields):
-                result[c, at, :] += gain * sums[w * height : (w + 1) * height, c * LANES : (c + 1) * LANES]
+                field[c, at, :] += gain * sums[w * height : (w + 1) * height, c * LANES : (c + 1) * LANES]
+
+    groups = columns // GROUP
+
+    def first_pass(g):
+        gains(g + 1)
+        for w in range(GROUP):
+            stencil(g * GROUP + w, f_a, f_b)
+
+    loop(columns, lambda cb: load_spring(cb).wait())
+    gains(0)
+    loop(groups - 1, first_pass)
+    for w in range(GROUP):
+        stencil((groups - 1) * GROUP + w, f_a, f_b)
+    for side in range(2):
+        gather(side, 0, matches, lambda at: g_ref[pl.ds(at, 1), :], put_g)
+
+    def edge_gain(way, cb, row):
+        edge_g[pl.ds(way * columns + cb, 1), :] = g_ref[pl.ds(row, 1), :]
+
+    each_edge(edge_gain)
 
     field, result = f_a, f_b
     for step in range(ITERS):
         last = step == ITERS - 1
-        stencil(field, result)
+        if step > 0:
+
+            def later_pass(g, field=field, result=result):
+                update(g + 1, field)
+                for w in range(GROUP):
+                    stencil(g * GROUP - 1 + w, field, result)
+
+            update(0, field)
+            loop(groups - 1, later_pass)
+            for w in range(GROUP + 1):
+                stencil((groups - 1) * GROUP - 1 + w, field, result)
         add_edges(step, result)
         for side in range(2):
             gather(side, 0, matches, rows_of(result), put_l)
+        if not last:
+
+            def edge_base(way, cb, row, step=step, result=result):
+                for c in range(fields):
+                    edge_out[step + 1, way, pl.ds(c * columns + cb, 1), :] = result[c, pl.ds(row, 1), :]
+
+            each_edge(edge_base)
         for chunk in range(CHUNKS):
             for side in range(2):
                 pl.when(neighbours[side][0])(row_copy(step, side, chunk, True).wait_recv)
-                first = side * matches + chunk * part
-                at = pl.ds(first, part)
+                at = pl.ds(side * matches + chunk * part, part)
+                first = (2 * chunk + side) * part
                 c = cmat[at, :]
                 for f in range(fields):
                     lanes = slice(f * LANES, (f + 1) * LANES)
                     high, low = split(c * (received[step, f, at, :] - sent[step, f, at, :]))
                     terms[first : first + part, lanes] = high
                     terms[both + first : both + first + part, lanes] = low
-        for chunk in range(CHUNKS):
-            for side in range(2):
-                at = pl.ds(side * matches + chunk * part, part)
-                sums = jnp.dot(pmat[at, :], terms[...], preferred_element_type=F32)
-                gain = gathered_g[at, :]
-                for f in range(fields):
-                    row = gathered_l[f, at, :] + gain * sums[:, f * LANES : (f + 1) * LANES]
-                    if last:
-                        last_rows[f, at, :] = row
-                    else:
-                        sent[step + 1, f, at, :] = row
-                if not last:
-                    send_rows(step + 1, side, chunk)
+            span = slice(2 * chunk * part, 2 * (chunk + 1) * part)
+            low_span = slice(both + span.start, both + span.stop)
+            for piece in range(CHUNKS):
+                for side in range(2):
+                    at = pl.ds(side * matches + piece * part, part)
+                    sums = jnp.dot(pmat[at, span], terms[span, :], preferred_element_type=F32)
+                    sums = sums + jnp.dot(pmat[at, span], terms[low_span, :], preferred_element_type=F32)
+                    if chunk > 0:
+                        sums = sums + partial[at, :]
+                    if chunk < CHUNKS - 1:
+                        partial[at, :] = sums
+                        continue
+                    gain = gathered_g[at, :]
+                    for f in range(fields):
+                        row = gathered_l[f, at, :] + gain * sums[:, f * LANES : (f + 1) * LANES]
+                        if last:
+                            last_rows[f, at, :] = row
+                        else:
+                            sent[step + 1, f, at, :] = row
+                    if not last:
+                        send_rows(step + 1, side, piece)
         if not last:
-            loop(columns // group, lambda g: update(g, result))
-            send_edges(step + 1, result)
+            sums = jnp.dot(edge_hot[...], terms[0:both, :], preferred_element_type=F32)
+            sums = sums + jnp.dot(edge_hot[...], terms[both:, :], preferred_element_type=F32)
+            for way in range(2):
+                here = slice(way * columns, (way + 1) * columns)
+                gain = edge_g[here, :]
+                for c in range(fields):
+                    edge_out[step + 1, way, c * columns : (c + 1) * columns, :] += (
+                        gain * sums[here, c * LANES : (c + 1) * LANES]
+                    )
+            send_edges(step + 1)
         field, result = result, field
 
     pl.when(has_next)(list_copy.wait_send)
@@ -354,7 +417,7 @@
                 pl.when(neighbours[side][0])(row_copy(step, side, chunk).wait_send)
 
 
-def finish(base, rows, index, out, field, scalar, index_sem, out_sem):
+def finish(base, rows, index, out, field, out_sem):
     fields, _, height, breadth = out.shape
     columns = breadth // LANES
     stride = height + PAD
@@ -373,7 +436,7 @@
         loop(matches // 16, group(side))
 
     def store(cb):
-        top = pl.multiple_of((cb + 1) * stride + PAD, PAD)
+        top = pl.multiple_of((cb + LEFT) * stride + PAD, PAD)
         lanes = pl.ds(pl.multiple_of(cb * LANES, LANES), LANES)
         return pltpu.make_async_copy(field.at[:, pl.ds(top, height), :], out.at[:, 0, :, lanes], out_sem.at[cb])
 
@@ -388,7 +451,7 @@
     both = 2 * matches
     width = fields * LANES
     vmem, smem, dma = pltpu.VMEM, pltpu.SMEM, pltpu.SemaphoreType.DMA
-    total = (columns + 2) * (height + PAD) + PAD
+    total = (columns + LEFT + 1) * (height + PAD) + PAD
     padded = (fields, total, LANES)
     anywhere = pl.BlockSpec(memory_space=pl.ANY)
     in_vmem, in_smem = pl.BlockSpec(memory_space=vmem), pl.BlockSpec(memory_space=smem)
@@ -406,10 +469,12 @@
             vmem((columns, height, LANES), F32),
             vmem((total, LANES), F32), vmem((total, LANES), F32),
             vmem((columns * height, both), BF16),
-            vmem((both, 2 * both), BF16),
+            vmem((both, both), BF16),
             smem(stiff_table.shape, F32),
             vmem((2, 1, matches), I32), vmem((2, 1, matches), I32), vmem((2, 1, matches), I32), vmem((2, 1, matches), I32),
-            vmem((both, LANES), F32), vmem((both, width), BF16), vmem((both, LANES), F32), vmem((both, LANES), F32),
+            vmem((both, LANES), F32), vmem((both, width), BF16), vmem((both, LANES), F32),
+            vmem((2 * columns, both), BF16), vmem((2 * columns, LANES), F32), vmem((both, width), F32),
+            vmem((both, LANES), F32),
             vmem((fields, both, LANES), F32),
             vmem((ITERS, fields, both, LANES), F32), vmem((ITERS, fields, both, LANES), F32),
             vmem((2 * both, width), BF16),
@@ -426,7 +491,7 @@
         out_shape=(jax.ShapeDtypeStruct(displacement.shape, F32), vmem(padded, F32)),
         in_specs=[in_vmem, in_vmem, in_smem],
         out_specs=(anywhere, in_vmem),
-        scratch_shapes=[smem((2, 1, matches), I32), dma, dma((columns,))],
+        scratch_shapes=[dma((columns,))],
         input_output_aliases={0: 1},
         compiler_params=pltpu.CompilerParams(vmem_limit_bytes=24 * 1024 * 1024),
     )(base, rows, index)

time: 46 us -> 40.7 us (0.88)
  Pallas kernels: 45.4 us -> 40.1 us
    pallas_call x1, Pallas kernels: 42.3 us -> 37.1 us  [on_device(): pl.pallas_call(relax, out_shape=(vmem(padded, F32), vmem((fields, both, L...]
where the time goes in v3:
time: 40.7 us; the launch traced here: 40.1 us
  Pallas kernels  40.1 us (99%)
    pallas_call x1, Pallas kernels, on_device(): pl.pallas_call(relax, out_shape=(vmem(padded, F32), vmem((fields, both, L...  37.1 us
    pallas_call x1, Pallas kernels, on_device(): pl.pallas_call(finish, out_shape=(jax.ShapeDtypeStruct(displacement.shape...  3.06 us

profile of v3, /device:TPU:8, one launch (start us, length us, event | category | flops | bytes accessed | tf_op | source)
XLA Modules:
  0.0 40.1 jit_solution(5981861401683332494)
XLA Ops:
  0.0 37.1 %shard_map.55 = (f32[2,5024,128]{2,1,0:T(8,128)S(1)}, f32[2,512,128]{2,1,0:T(8,128)S(1)}, s32[2,1,256]{2,1,0:T(1,128)S(4)}) custom-call(f32[2,1,256,2048]{3,2,1,0:T(8,128)} %disp.1, f32[1,256,2048]{2,1,0:T(8,128)} %spring.1, f32[8]{0:T(128)} %table_hbm.1, s32[2,1,256]{2,1,0:T(1,128)} %blocks.1, s32[1,256]{1,0:T(1,128)} %classes.1), custom_call_target="tpu_custom_call" | custom-call | tf_op jit(solution)/shard_map/pallas_call | solution.py:462
  37.1 3.1 %shard_map.56 = (f32[2,1,256,2048]{3,2,1,0:T(8,128)}, f32[2,5024,128]{2,1,0:T(8,128)S(1)}) custom-call(f32[2,5024,128]{2,1,0:T(8,128)S(1)} %get-tuple-element.9.base, f32[2,512,128]{2,1,0:T(8,128)S(1)} %get-tuple-element.10.rows, s32[2,1,256]{2,1,0:T(1,128)S(4)} %get-tuple-element.11.index), custom_call_target="tpu_custom_call", output_to_operand_aliasing={{1}: (0, {})} | custom-call | tf_op jit(solution)/shard_map/pallas_call | solution.py:489

commit v4 on v3

--- a/solution.py
+++ b/solution.py
@@ -35,11 +35,11 @@
     disp, spring, table_hbm, blocks, classes,
     f_b, last_rows, index,
     f_a, spr, a_ref, g_ref, onehot, pmat,
-    table, raw_blocks, lists_out, lists_in, lists_own,
+    table, own_raw, prev_raw, lists_in, lists_own,
     cmat, c_parts, block_cols, edge_hot, edge_g, partial, gathered_g, gathered_l, sent, received, terms,
     edge_out, edge_in,
     load_sem, spring_sem, list_sem, list_send, list_recv,
-    row_send, row_recv, edge_send, edge_recv,
+    row_send, row_recv, edge_send, edge_recv, ready,
 ):
     fields, _, height, breadth = disp.shape
     columns = breadth // LANES
@@ -58,23 +58,28 @@
         (has_lower, {"tile": tile + 1}),
     )
 
+    shift = columns.bit_length() - 1
+
     def first_row(cb):
         return pl.multiple_of((cb + LEFT) * stride + PAD, PAD)
 
     def lanes_of(cb):
         return pl.ds(pl.multiple_of(cb * LANES, LANES), LANES)
 
+    def signal(semaphore, peer):
+        pl.semaphore_signal(semaphore, inc=1, device_id=peer, device_id_type=MESH)
+
+    early, late = jnp.logical_and(has_lower, tile % 2 == 1), jnp.logical_and(has_upper, tile % 2 == 0)
     barrier = pltpu.get_barrier_semaphore()
-    for there, peer in neighbours:
-
-        @pl.when(there)
-        def _(peer=peer):
-            pl.semaphore_signal(barrier, inc=1, device_id=peer, device_id_type=MESH)
+    for i, (there, peer) in enumerate(neighbours):
+        greets = jnp.logical_and(there, jnp.logical_not(late)) if i == 2 else there
+        pl.when(greets)(lambda peer=peer: signal(barrier, peer))
 
     own_copies = [
-        pltpu.make_async_copy(blocks, raw_blocks, list_sem.at[0]),
-        pltpu.make_async_copy(classes, lists_own.at[1], list_sem.at[1]),
-        pltpu.make_async_copy(table_hbm, table, list_sem.at[2]),
+        pltpu.make_async_copy(blocks.at[0], own_raw, list_sem.at[0]),
+        pltpu.make_async_copy(blocks.at[0], lists_own.at[0], list_sem.at[1]),
+        pltpu.make_async_copy(classes, lists_own.at[1], list_sem.at[2]),
+        pltpu.make_async_copy(table_hbm, table, list_sem.at[3]),
     ]
     for copy in own_copies:
         copy.start()
@@ -88,6 +93,25 @@
         return pltpu.make_async_copy(spring.at[0, :, lanes_of(cb)], spr.at[cb], spring_sem.at[cb])
 
     loop(columns, lambda cb: load_field(cb).start())
+
+    awaited = [there.astype(I32) for there, _ in neighbours]
+    pl.semaphore_wait(barrier, sum(awaited) - early.astype(I32))
+    list_copies = [
+        pltpu.make_async_remote_copy(
+            src_ref=src, dst_ref=dst, send_sem=list_send.at[i], recv_sem=list_recv.at[i],
+            device_id={"sec": section + 1}, device_id_type=MESH,
+        )
+        for i, (src, dst) in enumerate(
+            ((blocks.at[1], prev_raw), (blocks.at[1], lists_in.at[0]), (classes, lists_in.at[1]))
+        )
+    ]
+
+    @pl.when(has_next)
+    def _():
+        for copy in list_copies:
+            copy.start()
+
+    pl.when(late)(lambda: signal(ready, neighbours[2][1]))
     loop(columns, lambda cb: load_spring(cb).start())
 
     zero_block = jnp.zeros((fields, stride, LANES), F32)
@@ -106,25 +130,8 @@
         def _(side=side):
             received[:, :, side * matches : (side + 1) * matches, :] = jnp.zeros((ITERS, fields, matches, LANES), F32)
 
-    for copy in own_copies:
-        copy.wait()
-
     def address(block):
         return (block % columns + LEFT) * stride + PAD + block // columns
-
-    lists_own[0] = address(raw_blocks[0])
-    lists_out[0] = address(raw_blocks[1])
-    lists_out[1] = lists_own[1]
-    own_scalar = pltpu.make_async_copy(lists_own.at[0], index.at[0], list_sem.at[0])
-    own_scalar.start()
-
-    pl.semaphore_wait(barrier, sum(there.astype(I32) for there, _ in neighbours))
-
-    list_copy = pltpu.make_async_remote_copy(
-        src_ref=lists_out, dst_ref=lists_in, send_sem=list_send, recv_sem=list_recv,
-        device_id={"sec": section + 1}, device_id_type=MESH,
-    )
-    pl.when(has_next)(list_copy.start)
 
     def edge_copy(step, way):
         return pltpu.make_async_remote_copy(
@@ -154,10 +161,17 @@
     def send_rows(step, side, chunk):
         pl.when(neighbours[side][0])(row_copy(step, side, chunk).start)
 
-    def gather(side, first, count, source, put):
+    def by_block(side, j):
+        block = (own_raw, prev_raw)[side][0, j]
+        return ((block & (columns - 1)) + LEFT) * stride + PAD + (block >> shift)
+
+    def by_address(side, j):
+        return index[side, 0, j]
+
+    def gather(side, first, count, source, put, find=by_address):
         def group(g):
             at = pl.multiple_of(first + g * 16, 16)
-            rows = [source(index[side, 0, at + j]) for j in range(16)]
+            rows = [source(find(side, at + j)) for j in range(16)]
             for j in range(16):
                 put(side * matches + at + j, rows[j])
 
@@ -175,10 +189,10 @@
     def put_g(at, row):
         gathered_g[pl.ds(at, 1), :] = row
 
-    own_scalar.wait()
+    own_copies[0].wait()
     loop(columns, lambda cb: load_field(cb).wait())
     for chunk in range(CHUNKS):
-        gather(0, chunk * part, part, rows_of(f_a), put_sent)
+        gather(0, chunk * part, part, rows_of(f_a), put_sent, by_block)
         send_rows(0, 0, chunk)
 
     def send_edges(step):
@@ -197,7 +211,11 @@
             edge_out[0, way, pl.ds(c * columns + cb, 1), :] = f_a[c, pl.ds(row, 1), :]
 
     each_edge(first_edge)
-    send_edges(0)
+    for copy in own_copies[1:]:
+        copy.wait()
+    lists_own[0] = address(lists_own[0])
+    own_scalar = pltpu.make_async_copy(lists_own.at[0], index.at[0], list_sem.at[0])
+    own_scalar.start()
 
     def stiffness(lists, alive):
         kind = lists[1]
@@ -242,18 +260,35 @@
 
     @pl.when(has_prev)
     def _():
-        list_copy.wait_recv()
+        list_copies[0].wait_recv()
 
     @pl.when(jnp.logical_not(has_prev))
     def _():
-        lists_in[...] = lists_out[...]
-
-    prev_scalar = pltpu.make_async_copy(lists_in.at[0], index.at[1], list_sem.at[0])
+        copies = [
+            pltpu.make_async_copy(src, dst, list_sem.at[1 + i])
+            for i, (src, dst) in enumerate(
+                ((blocks.at[1], prev_raw), (blocks.at[1], lists_in.at[0]), (classes, lists_in.at[1]))
+            )
+        ]
+        for copy in copies:
+            copy.start()
+        for copy in copies:
+            copy.wait()
+
+    for chunk in range(CHUNKS):
+        gather(1, chunk * part, part, rows_of(f_a), put_sent, by_block)
+        send_rows(0, 1, chunk)
+    pl.when(early)(lambda: pl.semaphore_wait(ready, 1))
+    send_edges(0)
+
+    @pl.when(has_prev)
+    def _():
+        list_copies[1].wait_recv()
+        list_copies[2].wait_recv()
+
+    lists_in[0] = address(lists_in[0])
+    prev_scalar = pltpu.make_async_copy(lists_in.at[0], index.at[1], list_sem.at[1])
     prev_scalar.start()
-    prev_scalar.wait()
-    for chunk in range(CHUNKS):
-        gather(1, chunk * part, part, rows_of(f_a), put_sent)
-        send_rows(0, 1, chunk)
     fill_side(1, lists_in, has_prev)
 
     def fill_pmat(g):
@@ -331,6 +366,8 @@
     loop(groups - 1, first_pass)
     for w in range(GROUP):
         stencil((groups - 1) * GROUP + w, f_a, f_b)
+    own_scalar.wait()
+    prev_scalar.wait()
     for side in range(2):
         gather(side, 0, matches, lambda at: g_ref[pl.ds(at, 1), :], put_g)
 
@@ -408,7 +445,11 @@
             send_edges(step + 1)
         field, result = result, field
 
-    pl.when(has_next)(list_copy.wait_send)
+    @pl.when(has_next)
+    def _():
+        for copy in list_copies:
+            copy.wait_send()
+
     for step in range(ITERS):
         for way in range(2):
             pl.when(neighbours[2 + way][0])(edge_copy(step, way).wait_send)
@@ -423,25 +464,24 @@
     stride = height + PAD
     matches = index.shape[2]
 
-    def group(side):
-        def one(g):
-            at = pl.multiple_of(g * 16, 16)
-            got = [rows[:, pl.ds(side * matches + at + j, 1), :] for j in range(16)]
-            for j in range(16):
-                field[:, pl.ds(index[side, 0, at + j], 1), :] = got[j]
-
-        return one
-
-    for side in range(2):
-        loop(matches // 16, group(side))
-
-    def store(cb):
+    def store(c, cb):
         top = pl.multiple_of((cb + LEFT) * stride + PAD, PAD)
         lanes = pl.ds(pl.multiple_of(cb * LANES, LANES), LANES)
-        return pltpu.make_async_copy(field.at[:, pl.ds(top, height), :], out.at[:, 0, :, lanes], out_sem.at[cb])
-
-    loop(columns, lambda cb: store(cb).start())
-    loop(columns, lambda cb: store(cb).wait())
+        return pltpu.make_async_copy(field.at[c, pl.ds(top, height), :], out.at[c, 0, :, lanes], out_sem.at[c, cb])
+
+    for c in range(fields):
+        for side in range(2):
+
+            def group(g, c=c, side=side):
+                at = pl.multiple_of(g * 32, 32)
+                got = [rows[c, pl.ds(side * matches + at + j, 1), :] for j in range(32)]
+                for j in range(32):
+                    field[c, pl.ds(index[side, 0, at + j], 1), :] = got[j]
+
+            loop(matches // 32, group)
+        loop(columns, lambda cb: store(c, cb).start())
+    for c in range(fields):
+        loop(columns, lambda cb: store(c, cb).wait())
 
 
 def on_device(displacement, spring, stiff_table, match_blocks, match_class):
@@ -471,7 +511,7 @@
             vmem((columns * height, both), BF16),
             vmem((both, both), BF16),
             smem(stiff_table.shape, F32),
-            vmem((2, 1, matches), I32), vmem((2, 1, matches), I32), vmem((2, 1, matches), I32), vmem((2, 1, matches), I32),
+            smem((1, matches), I32), smem((1, matches), I32), vmem((2, 1, matches), I32), vmem((2, 1, matches), I32),
             vmem((both, LANES), F32), vmem((both, width), BF16), vmem((both, LANES), F32),
             vmem((2 * columns, both), BF16), vmem((2 * columns, LANES), F32), vmem((both, width), F32),
             vmem((both, LANES), F32),
@@ -479,8 +519,9 @@
             vmem((ITERS, fields, both, LANES), F32), vmem((ITERS, fields, both, LANES), F32),
             vmem((2 * both, width), BF16),
             vmem((ITERS, 2, fields * columns, LANES), F32), vmem((ITERS, 2, fields * columns, LANES), F32),
-            dma((columns,)), dma((columns,)), dma((3,)), dma, dma,
+            dma((columns,)), dma((columns,)), dma((4,)), dma((3,)), dma((3,)),
             dma((ITERS, 2, CHUNKS)), dma((ITERS, 2, CHUNKS)), dma((ITERS, 2)), dma((ITERS, 2)),
+            pltpu.SemaphoreType.REGULAR,
         ],
         compiler_params=pltpu.CompilerParams(
             collective_id=0, has_side_effects=True, vmem_limit_bytes=48 * 1024 * 1024
@@ -491,7 +532,7 @@
         out_shape=(jax.ShapeDtypeStruct(displacement.shape, F32), vmem(padded, F32)),
         in_specs=[in_vmem, in_vmem, in_smem],
         out_specs=(anywhere, in_vmem),
-        scratch_shapes=[dma((columns,))],
+        scratch_shapes=[dma((fields, columns))],
         input_output_aliases={0: 1},
         compiler_params=pltpu.CompilerParams(vmem_limit_bytes=24 * 1024 * 1024),
     )(base, rows, index)

time: 40.7 us -> 39.7 us (0.975); the launches traced: 40.1 us -> 39.5 us
  Pallas kernels: 40.1 us -> 39.5 us
    pallas_call x1, Pallas kernels: 37.1 us -> 36.2 us  [on_device(): pl.pallas_call(relax, out_shape=(vmem(padded, F32), vmem((fields, both, L...]
where the time goes in v4:
time: 39.7 us; the launch traced here: 39.5 us
  Pallas kernels  39.5 us (99%)
    pallas_call x1, Pallas kernels, on_device(): pl.pallas_call(relax, out_shape=(vmem(padded, F32), vmem((fields, both, L...  36.2 us
    pallas_call x1, Pallas kernels, on_device(): pl.pallas_call(finish, out_shape=(jax.ShapeDtypeStruct(displacement.shape...  3.36 us

profile of v4, /device:TPU:8, one launch (start us, length us, event | category | flops | bytes accessed | tf_op | source)
XLA Modules:
  0.0 39.5 jit_solution(9647697047008740719)
XLA Ops:
  0.0 36.2 %shard_map.55 = (f32[2,5024,128]{2,1,0:T(8,128)S(1)}, f32[2,512,128]{2,1,0:T(8,128)S(1)}, s32[2,1,256]{2,1,0:T(1,128)S(4)}) custom-call(f32[2,1,256,2048]{3,2,1,0:T(8,128)} %disp.1, f32[1,256,2048]{2,1,0:T(8,128)} %spring.1, f32[8]{0:T(128)} %table_hbm.1, s32[2,1,256]{2,1,0:T(1,128)} %blocks.1, s32[1,256]{1,0:T(1,128)} %classes.1), custom_call_target="tpu_custom_call" | custom-call | tf_op jit(solution)/shard_map/pallas_call | solution.py:502
  36.2 3.4 %shard_map.56 = (f32[2,1,256,2048]{3,2,1,0:T(8,128)}, f32[2,5024,128]{2,1,0:T(8,128)S(1)}) custom-call(f32[2,5024,128]{2,1,0:T(8,128)S(1)} %get-tuple-element.9.base, f32[2,512,128]{2,1,0:T(8,128)S(1)} %get-tuple-element.10.rows, s32[2,1,256]{2,1,0:T(1,128)S(4)} %get-tuple-element.11.index), custom_call_target="tpu_custom_call", output_to_operand_aliasing={{1}: (0, {})} | custom-call | tf_op jit(solution)/shard_map/pallas_call | solution.py:530

commit v5 on v4

--- a/solution.py
+++ b/solution.py
@@ -35,11 +35,11 @@
     disp, spring, table_hbm, blocks, classes,
     f_b, last_rows, index,
     f_a, spr, a_ref, g_ref, onehot, pmat,
-    table, own_raw, prev_raw, lists_in, lists_own,
-    cmat, c_parts, block_cols, edge_hot, edge_g, partial, gathered_g, gathered_l, sent, received, terms,
+    table, own_raw, prev_raw, lists_in, lists_own, places,
+    cmat, c_parts, block_cols, far_cols, edge_hot, edge_g, far_pmat, far_g, far_sums, mine, gathered_g, gathered_l, sent, received, terms,
     edge_out, edge_in,
     load_sem, spring_sem, list_sem, list_send, list_recv,
-    row_send, row_recv, edge_send, edge_recv, ready,
+    row_send, row_recv, edge_send, edge_recv, gain_send, gain_recv, ready,
 ):
     fields, _, height, breadth = disp.shape
     columns = breadth // LANES
@@ -77,8 +77,8 @@
 
     own_copies = [
         pltpu.make_async_copy(blocks.at[0], own_raw, list_sem.at[0]),
-        pltpu.make_async_copy(blocks.at[0], lists_own.at[0], list_sem.at[1]),
-        pltpu.make_async_copy(classes, lists_own.at[1], list_sem.at[2]),
+        pltpu.make_async_copy(blocks, lists_own.at[0:2], list_sem.at[1]),
+        pltpu.make_async_copy(classes, lists_own.at[2], list_sem.at[2]),
         pltpu.make_async_copy(table_hbm, table, list_sem.at[3]),
     ]
     for copy in own_copies:
@@ -90,7 +90,9 @@
         )
 
     def load_spring(cb):
-        return pltpu.make_async_copy(spring.at[0, :, lanes_of(cb)], spr.at[cb], spring_sem.at[cb])
+        return pltpu.make_async_copy(
+            spring.at[0, :, lanes_of(cb)], spr.at[pl.ds(first_row(cb), height), :], spring_sem.at[cb]
+        )
 
     loop(columns, lambda cb: load_field(cb).start())
 
@@ -102,7 +104,7 @@
             device_id={"sec": section + 1}, device_id_type=MESH,
         )
         for i, (src, dst) in enumerate(
-            ((blocks.at[1], prev_raw), (blocks.at[1], lists_in.at[0]), (classes, lists_in.at[1]))
+            ((blocks.at[1], prev_raw), (blocks, lists_in.at[0:2]), (classes, lists_in.at[2]))
         )
     ]
 
@@ -129,6 +131,7 @@
         @pl.when(jnp.logical_not(there))
         def _(side=side):
             received[:, :, side * matches : (side + 1) * matches, :] = jnp.zeros((ITERS, fields, matches, LANES), F32)
+            far_g[side * matches : (side + 1) * matches, :] = jnp.zeros((matches, LANES), F32)
 
     def address(block):
         return (block % columns + LEFT) * stride + PAD + block // columns
@@ -213,24 +216,26 @@
     each_edge(first_edge)
     for copy in own_copies[1:]:
         copy.wait()
-    lists_own[0] = address(lists_own[0])
-    own_scalar = pltpu.make_async_copy(lists_own.at[0], index.at[0], list_sem.at[0])
+    places[0] = address(lists_own[0])
+    own_scalar = pltpu.make_async_copy(places.at[0], index.at[0], list_sem.at[0])
     own_scalar.start()
 
     def stiffness(lists, alive):
-        kind = lists[1]
+        kind = lists[2]
         stiff = jnp.zeros(kind.shape, F32)
         for level in range(table.shape[0]):
             stiff = jnp.where(kind == level, table[level], stiff)
         return stiff * jnp.where(alive, 1.0, 0.0)
 
     def place(side, j):
-        first = j * LANES // part * 2 * part + side * part + j * LANES % part
+        first = side * matches + j * LANES
         return slice(first, first + LANES)
 
-    def fill_side(side, lists, alive):
+    def columns_of(wanted):
+        return jnp.transpose(jnp.broadcast_to(wanted.astype(F32), (LANES, matches)))
+
+    def fill_small(side, lists, alive):
         half = pl.ds(side * matches, matches)
-        wanted = lists[0]
         stiff = jnp.transpose(jnp.broadcast_to(stiffness(lists, alive), (LANES, matches)))
         cmat[half, :] = stiff
         high, low = split(stiff)
@@ -238,7 +243,11 @@
             from_rows = slice(j * LANES, (j + 1) * LANES)
             c_parts[place(side, j), 0:LANES] = high[from_rows]
             c_parts[place(side, j), LANES:] = low[from_rows]
-        block_cols[half, :] = jnp.transpose(jnp.broadcast_to(wanted.astype(F32), (LANES, matches)))
+        block_cols[half, :] = columns_of(lists[side])
+        far_cols[half, :] = columns_of(lists[1 - side])
+
+    def fill_large(side):
+        wanted = places[side]
 
         def hits(row, j):
             hit = row == wanted[:, j * LANES : (j + 1) * LANES]
@@ -256,7 +265,8 @@
         for j in range(matches // LANES):
             edge_hot[:, place(side, j)] = hits(row, j)
 
-    fill_side(0, lists_own, has_next)
+    fill_small(0, lists_own, has_next)
+    fill_large(0)
 
     @pl.when(has_prev)
     def _():
@@ -267,7 +277,7 @@
         copies = [
             pltpu.make_async_copy(src, dst, list_sem.at[1 + i])
             for i, (src, dst) in enumerate(
-                ((blocks.at[1], prev_raw), (blocks.at[1], lists_in.at[0]), (classes, lists_in.at[1]))
+                ((blocks.at[1], prev_raw), (blocks, lists_in.at[0:2]), (classes, lists_in.at[2]))
             )
         ]
         for copy in copies:
@@ -286,21 +296,53 @@
         list_copies[1].wait_recv()
         list_copies[2].wait_recv()
 
-    lists_in[0] = address(lists_in[0])
-    prev_scalar = pltpu.make_async_copy(lists_in.at[0], index.at[1], list_sem.at[1])
+    places[1] = address(lists_in[1])
+    prev_scalar = pltpu.make_async_copy(places.at[1], index.at[1], list_sem.at[1])
     prev_scalar.start()
-    fill_side(1, lists_in, has_prev)
+    fill_small(1, lists_in, has_prev)
+
+    def hits_of(col, row):
+        return jnp.where(col == row, 1.0, 0.0).astype(BF16)
 
     def fill_pmat(g):
         at = pl.ds(pl.multiple_of(g * STRIP, STRIP), STRIP)
         col = block_cols[at, :]
         for side, lists in enumerate((lists_own, lists_in)):
-            row = lists[0].astype(F32)
+            row = lists[side].astype(F32)
             for j in range(matches // LANES):
-                hit = jnp.where(col == row[:, j * LANES : (j + 1) * LANES], 1.0, 0.0).astype(BF16)
-                pmat[at, place(side, j)] = hit
+                pmat[at, place(side, j)] = hits_of(col, row[:, j * LANES : (j + 1) * LANES])
+
+    def fill_far(g):
+        at = pl.ds(pl.multiple_of(g * STRIP, STRIP), STRIP)
+        for side, lists in enumerate((lists_own, lists_in)):
+            row = lists[1 - side].astype(F32)
+            rows = pl.ds(pl.multiple_of(side * matches + g * STRIP, STRIP), STRIP)
+            col = far_cols[rows, :]
+            for j in range(matches // LANES):
+                far_pmat[rows, j * LANES : (j + 1) * LANES] = hits_of(col, row[:, j * LANES : (j + 1) * LANES])
 
     loop(both // STRIP, fill_pmat)
+    loop(columns, lambda cb: load_spring(cb).wait())
+    own_scalar.wait()
+    prev_scalar.wait()
+    for side in range(2):
+        gather(side, 0, matches, lambda at: spr[pl.ds(at, 1), :], put_g)
+    sums = jnp.dot(pmat[...], c_parts[...], preferred_element_type=F32)
+    gathered_g[...] = 0.8 / (4.0 * gathered_g[...] + (sums[:, :LANES] + sums[:, LANES:]))
+
+    def gain_copy(side, arrival=False):
+        theirs = side if arrival else 1 - side
+        return pltpu.make_async_remote_copy(
+            src_ref=gathered_g.at[pl.ds(side * matches, matches), :],
+            dst_ref=far_g.at[pl.ds(theirs * matches, matches), :],
+            send_sem=gain_send.at[side], recv_sem=gain_recv.at[theirs],
+            device_id=neighbours[side][1], device_id_type=MESH,
+        )
+
+    for side in range(2):
+        pl.when(neighbours[side][0])(gain_copy(side).start)
+    fill_large(1)
+    loop(matches // STRIP, fill_far)
 
     def gains(g):
         at = pl.ds(pl.multiple_of(g * GROUP * height, GROUP * height), GROUP * height)
@@ -308,9 +350,9 @@
         for w in range(GROUP):
             cb = g * GROUP + w
             here = sums[w * height : (w + 1) * height]
-            stiff = spr[cb]
+            at = pl.ds(first_row(cb), height)
+            stiff = spr[at, :]
             gain = 0.8 / (4.0 * stiff + (here[:, :LANES] + here[:, LANES:]))
-            at = pl.ds(first_row(cb), height)
             g_ref[at, :] = gain
             a_ref[at, :] = gain * stiff
 
@@ -361,20 +403,20 @@
         for w in range(GROUP):
             stencil(g * GROUP + w, f_a, f_b)
 
-    loop(columns, lambda cb: load_spring(cb).wait())
     gains(0)
     loop(groups - 1, first_pass)
     for w in range(GROUP):
         stencil((groups - 1) * GROUP + w, f_a, f_b)
-    own_scalar.wait()
-    prev_scalar.wait()
-    for side in range(2):
-        gather(side, 0, matches, lambda at: g_ref[pl.ds(at, 1), :], put_g)
-
     def edge_gain(way, cb, row):
         edge_g[pl.ds(way * columns + cb, 1), :] = g_ref[pl.ds(row, 1), :]
 
     each_edge(edge_gain)
+
+    def product(chosen, side):
+        first = side * matches
+        sums = jnp.dot(chosen, terms[first : first + matches, :], preferred_element_type=F32)
+        first = both + first
+        return sums + jnp.dot(chosen, terms[first : first + matches, :], preferred_element_type=F32)
 
     field, result = f_a, f_b
     for step in range(ITERS):
@@ -400,38 +442,41 @@
                     edge_out[step + 1, way, pl.ds(c * columns + cb, 1), :] = result[c, pl.ds(row, 1), :]
 
             each_edge(edge_base)
-        for chunk in range(CHUNKS):
+        if step > 0:
             for side in range(2):
+                if step == 1:
+                    pl.when(neighbours[side][0])(gain_copy(side, True).wait_recv)
+                half = pl.ds(side * matches, matches)
+                sums = product(far_pmat[half, :], side)
+                for f in range(fields):
+                    far_sums[f, half, :] = far_g[half, :] * sums[:, f * LANES : (f + 1) * LANES]
+        for side in (1, 0):
+            for chunk in range(CHUNKS):
                 pl.when(neighbours[side][0])(row_copy(step, side, chunk, True).wait_recv)
-                at = pl.ds(side * matches + chunk * part, part)
-                first = (2 * chunk + side) * part
+                first = side * matches + chunk * part
+                at = pl.ds(first, part)
                 c = cmat[at, :]
                 for f in range(fields):
                     lanes = slice(f * LANES, (f + 1) * LANES)
-                    high, low = split(c * (received[step, f, at, :] - sent[step, f, at, :]))
+                    there, here = received[step, f, at, :], sent[0, f, at, :] if step == 0 else mine[f, at, :]
+                    if step > 0:
+                        there = there - far_sums[f, at, :]
+                    high, low = split(c * (there - here))
                     terms[first : first + part, lanes] = high
                     terms[both + first : both + first + part, lanes] = low
-            span = slice(2 * chunk * part, 2 * (chunk + 1) * part)
-            low_span = slice(both + span.start, both + span.stop)
-            for piece in range(CHUNKS):
-                for side in range(2):
-                    at = pl.ds(side * matches + piece * part, part)
-                    sums = jnp.dot(pmat[at, span], terms[span, :], preferred_element_type=F32)
-                    sums = sums + jnp.dot(pmat[at, span], terms[low_span, :], preferred_element_type=F32)
-                    if chunk > 0:
-                        sums = sums + partial[at, :]
-                    if chunk < CHUNKS - 1:
-                        partial[at, :] = sums
-                        continue
-                    gain = gathered_g[at, :]
-                    for f in range(fields):
-                        row = gathered_l[f, at, :] + gain * sums[:, f * LANES : (f + 1) * LANES]
-                        if last:
-                            last_rows[f, at, :] = row
-                        else:
-                            sent[step + 1, f, at, :] = row
-                    if not last:
-                        send_rows(step + 1, side, piece)
+            across = slice(side * matches, (side + 1) * matches)
+            for chunk in range(CHUNKS):
+                at = pl.ds((1 - side) * matches + chunk * part, part)
+                sums = product(pmat[at, across], side)
+                gain = gathered_g[at, :]
+                for f in range(fields):
+                    row = gathered_l[f, at, :] + gain * sums[:, f * LANES : (f + 1) * LANES]
+                    if last:
+                        last_rows[f, at, :] = row
+                    else:
+                        sent[step + 1, f, at, :] = row
+                if not last:
+                    send_rows(step + 1, 1 - side, chunk)
         if not last:
             sums = jnp.dot(edge_hot[...], terms[0:both, :], preferred_element_type=F32)
             sums = sums + jnp.dot(edge_hot[...], terms[both:, :], preferred_element_type=F32)
@@ -443,6 +488,16 @@
                         gain * sums[here, c * LANES : (c + 1) * LANES]
                     )
             send_edges(step + 1)
+        for side in range(2):
+            half = slice(side * matches, (side + 1) * matches)
+            sums = product(pmat[half, half], side)
+            gain = gathered_g[half, :]
+            for f in range(fields):
+                add = gain * sums[:, f * LANES : (f + 1) * LANES]
+                if last:
+                    last_rows[f, half, :] += add
+                else:
+                    mine[f, half, :] = sent[step + 1, f, half, :] + add
         field, result = result, field
 
     @pl.when(has_next)
@@ -450,6 +505,8 @@
         for copy in list_copies:
             copy.wait_send()
 
+    for side in range(2):
+        pl.when(neighbours[side][0])(gain_copy(side).wait_send)
     for step in range(ITERS):
         for way in range(2):
             pl.when(neighbours[2 + way][0])(edge_copy(step, way).wait_send)
@@ -464,24 +521,25 @@
     stride = height + PAD
     matches = index.shape[2]
 
-    def store(c, cb):
+    def group(side):
+        def one(g):
+            at = pl.multiple_of(g * 16, 16)
+            got = [rows[:, pl.ds(side * matches + at + j, 1), :] for j in range(16)]
+            for j in range(16):
+                field[:, pl.ds(index[side, 0, at + j], 1), :] = got[j]
+
+        return one
+
+    for side in range(2):
+        loop(matches // 16, group(side))
+
+    def store(cb):
         top = pl.multiple_of((cb + LEFT) * stride + PAD, PAD)
         lanes = pl.ds(pl.multiple_of(cb * LANES, LANES), LANES)
-        return pltpu.make_async_copy(field.at[c, pl.ds(top, height), :], out.at[c, 0, :, lanes], out_sem.at[c, cb])
-
-    for c in range(fields):
-        for side in range(2):
-
-            def group(g, c=c, side=side):
-                at = pl.multiple_of(g * 32, 32)
-                got = [rows[c, pl.ds(side * matches + at + j, 1), :] for j in range(32)]
-                for j in range(32):
-                    field[c, pl.ds(index[side, 0, at + j], 1), :] = got[j]
-
-            loop(matches // 32, group)
-        loop(columns, lambda cb: store(c, cb).start())
-    for c in range(fields):
-        loop(columns, lambda cb: store(c, cb).wait())
+        return pltpu.make_async_copy(field.at[:, pl.ds(top, height), :], out.at[:, 0, :, lanes], out_sem.at[cb])
+
+    loop(columns, lambda cb: store(cb).start())
+    loop(columns, lambda cb: store(cb).wait())
 
 
 def on_device(displacement, spring, stiff_table, match_blocks, match_class):
@@ -506,21 +564,21 @@
         out_specs=(in_vmem, in_vmem, in_smem),
         scratch_shapes=[
             vmem(padded, F32),
-            vmem((columns, height, LANES), F32),
-            vmem((total, LANES), F32), vmem((total, LANES), F32),
+            vmem((total, LANES), F32), vmem((total, LANES), F32), vmem((total, LANES), F32),
             vmem((columns * height, both), BF16),
             vmem((both, both), BF16),
             smem(stiff_table.shape, F32),
-            smem((1, matches), I32), smem((1, matches), I32), vmem((2, 1, matches), I32), vmem((2, 1, matches), I32),
-            vmem((both, LANES), F32), vmem((both, width), BF16), vmem((both, LANES), F32),
-            vmem((2 * columns, both), BF16), vmem((2 * columns, LANES), F32), vmem((both, width), F32),
+            smem((1, matches), I32), smem((1, matches), I32), vmem((3, 1, matches), I32), vmem((3, 1, matches), I32), vmem((2, 1, matches), I32),
+            vmem((both, LANES), F32), vmem((both, width), BF16), vmem((both, LANES), F32), vmem((both, LANES), F32),
+            vmem((2 * columns, both), BF16), vmem((2 * columns, LANES), F32), vmem((both, matches), BF16),
+            vmem((both, LANES), F32), vmem((fields, both, LANES), F32), vmem((fields, both, LANES), F32),
             vmem((both, LANES), F32),
             vmem((fields, both, LANES), F32),
             vmem((ITERS, fields, both, LANES), F32), vmem((ITERS, fields, both, LANES), F32),
             vmem((2 * both, width), BF16),
             vmem((ITERS, 2, fields * columns, LANES), F32), vmem((ITERS, 2, fields * columns, LANES), F32),
             dma((columns,)), dma((columns,)), dma((4,)), dma((3,)), dma((3,)),
-            dma((ITERS, 2, CHUNKS)), dma((ITERS, 2, CHUNKS)), dma((ITERS, 2)), dma((ITERS, 2)),
+            dma((ITERS, 2, CHUNKS)), dma((ITERS, 2, CHUNKS)), dma((ITERS, 2)), dma((ITERS, 2)), dma((2,)), dma((2,)),
             pltpu.SemaphoreType.REGULAR,
         ],
         compiler_params=pltpu.CompilerParams(
@@ -532,7 +590,7 @@
         out_shape=(jax.ShapeDtypeStruct(displacement.shape, F32), vmem(padded, F32)),
         in_specs=[in_vmem, in_vmem, in_smem],
         out_specs=(anywhere, in_vmem),
-        scratch_shapes=[dma((fields, columns))],
+        scratch_shapes=[dma((columns,))],
         input_output_aliases={0: 1},
         compiler_params=pltpu.CompilerParams(vmem_limit_bytes=24 * 1024 * 1024),
     )(base, rows, index)

time: 39.7 us -> 45.8 us (1.15)
  the two profiles are of different devices: /device:TPU:8 before, /device:TPU:15 now
where the time goes in v5:
time: 45.8 us; the launch traced here: 45.7 us
  Pallas kernels  45.7 us (100%)
    pallas_call x1, Pallas kernels, on_device(): pl.pallas_call(relax, out_shape=(vmem(padded, F32), vmem((fields, both, L...  42.6 us
    pallas_call x1, Pallas kernels, on_device(): pl.pallas_call(finish, out_shape=(jax.ShapeDtypeStruct(displacement.shape...  3.06 us

profile of v5, /device:TPU:15, one launch (start us, length us, event | category | flops | bytes accessed | tf_op | source)
XLA Modules:
  0.0 45.7 jit_solution(4405481548854837188)
XLA Ops:
  0.0 42.6 %shard_map.55 = (f32[2,5024,128]{2,1,0:T(8,128)S(1)}, f32[2,512,128]{2,1,0:T(8,128)S(1)}, s32[2,1,256]{2,1,0:T(1,128)S(4)}) custom-call(f32[2,1,256,2048]{3,2,1,0:T(8,128)} %disp.1, f32[1,256,2048]{2,1,0:T(8,128)} %spring.1, f32[8]{0:T(128)} %table_hbm.1, s32[2,1,256]{2,1,0:T(1,128)} %blocks.1, s32[1,256]{1,0:T(1,128)} %classes.1), custom_call_target="tpu_custom_call" | custom-call | tf_op jit(solution)/shard_map/pallas_call | solution.py:560
  42.6 3.1 %shard_map.56 = (f32[2,1,256,2048]{3,2,1,0:T(8,128)}, f32[2,5024,128]{2,1,0:T(8,128)S(1)}) custom-call(f32[2,5024,128]{2,1,0:T(8,128)S(1)} %get-tuple-element.9.base, f32[2,512,128]{2,1,0:T(8,128)S(1)} %get-tuple-element.10.rows, s32[2,1,256]{2,1,0:T(1,128)S(4)} %get-tuple-element.11.index), custom_call_target="tpu_custom_call", output_to_operand_aliasing={{1}: (0, {})} | custom-call | tf_op jit(solution)/shard_map/pallas_call | solution.py:588

commit v6 on v4

--- a/solution.py
+++ b/solution.py
@@ -81,9 +81,6 @@
         pltpu.make_async_copy(classes, lists_own.at[1], list_sem.at[2]),
         pltpu.make_async_copy(table_hbm, table, list_sem.at[3]),
     ]
-    for copy in own_copies:
-        copy.start()
-
     def load_field(cb):
         return pltpu.make_async_copy(
             disp.at[:, 0, :, lanes_of(cb)], f_a.at[:, pl.ds(first_row(cb), height), :], load_sem.at[cb]
@@ -92,7 +89,6 @@
     def load_spring(cb):
         return pltpu.make_async_copy(spring.at[0, :, lanes_of(cb)], spr.at[cb], spring_sem.at[cb])
 
-    loop(columns, lambda cb: load_field(cb).start())
 
     awaited = [there.astype(I32) for there, _ in neighbours]
     pl.semaphore_wait(barrier, sum(awaited) - early.astype(I32))
@@ -112,6 +108,9 @@
             copy.start()
 
     pl.when(late)(lambda: signal(ready, neighbours[2][1]))
+    for copy in own_copies:
+        copy.start()
+    loop(columns, lambda cb: load_field(cb).start())
     loop(columns, lambda cb: load_spring(cb).start())
 
     zero_block = jnp.zeros((fields, stride, LANES), F32)
@@ -464,24 +463,25 @@
     stride = height + PAD
     matches = index.shape[2]
 
-    def store(c, cb):
+    def group(side):
+        def one(g):
+            at = pl.multiple_of(g * 16, 16)
+            got = [rows[:, pl.ds(side * matches + at + j, 1), :] for j in range(16)]
+            for j in range(16):
+                field[:, pl.ds(index[side, 0, at + j], 1), :] = got[j]
+
+        return one
+
+    for side in range(2):
+        loop(matches // 16, group(side))
+
+    def store(cb):
         top = pl.multiple_of((cb + LEFT) * stride + PAD, PAD)
         lanes = pl.ds(pl.multiple_of(cb * LANES, LANES), LANES)
-        return pltpu.make_async_copy(field.at[c, pl.ds(top, height), :], out.at[c, 0, :, lanes], out_sem.at[c, cb])
-
-    for c in range(fields):
-        for side in range(2):
-
-            def group(g, c=c, side=side):
-                at = pl.multiple_of(g * 32, 32)
-                got = [rows[c, pl.ds(side * matches + at + j, 1), :] for j in range(32)]
-                for j in range(32):
-                    field[c, pl.ds(index[side, 0, at + j], 1), :] = got[j]
-
-            loop(matches // 32, group)
-        loop(columns, lambda cb: store(c, cb).start())
-    for c in range(fields):
-        loop(columns, lambda cb: store(c, cb).wait())
+        return pltpu.make_async_copy(field.at[:, pl.ds(top, height), :], out.at[:, 0, :, lanes], out_sem.at[cb])
+
+    loop(columns, lambda cb: store(cb).start())
+    loop(columns, lambda cb: store(cb).wait())
 
 
 def on_device(displacement, spring, stiff_table, match_blocks, match_class):
@@ -532,7 +532,7 @@
         out_shape=(jax.ShapeDtypeStruct(displacement.shape, F32), vmem(padded, F32)),
         in_specs=[in_vmem, in_vmem, in_smem],
         out_specs=(anywhere, in_vmem),
-        scratch_shapes=[dma((fields, columns))],
+        scratch_shapes=[dma((columns,))],
         input_output_aliases={0: 1},
         compiler_params=pltpu.CompilerParams(vmem_limit_bytes=24 * 1024 * 1024),
     )(base, rows, index)

time: 39.7 us -> 41.1 us (1.035)
  Pallas kernels: 39.5 us -> 41 us
    pallas_call x1, Pallas kernels: 36.2 us -> 37.9 us  [on_device(): pl.pallas_call(relax, out_shape=(vmem(padded, F32), vmem((fields, both, L...]
where the time goes in v6:
time: 41.1 us; the launch traced here: 41 us
  Pallas kernels  41 us (100%)
    pallas_call x1, Pallas kernels, on_device(): pl.pallas_call(relax, out_shape=(vmem(padded, F32), vmem((fields, both, L...  37.9 us
    pallas_call x1, Pallas kernels, on_device(): pl.pallas_call(finish, out_shape=(jax.ShapeDtypeStruct(displacement.shape...  3.06 us

profile of v6, /device:TPU:8, one launch (start us, length us, event | category | flops | bytes accessed | tf_op | source)
XLA Modules:
  0.0 41.0 jit_solution(7262688067731061564)
XLA Ops:
  0.0 37.9 %shard_map.55 = (f32[2,5024,128]{2,1,0:T(8,128)S(1)}, f32[2,512,128]{2,1,0:T(8,128)S(1)}, s32[2,1,256]{2,1,0:T(1,128)S(4)}) custom-call(f32[2,1,256,2048]{3,2,1,0:T(8,128)} %disp.1, f32[1,256,2048]{2,1,0:T(8,128)} %spring.1, f32[8]{0:T(128)} %table_hbm.1, s32[2,1,256]{2,1,0:T(1,128)} %blocks.1, s32[1,256]{1,0:T(1,128)} %classes.1), custom_call_target="tpu_custom_call" | custom-call | tf_op jit(solution)/shard_map/pallas_call | solution.py:502
  37.9 3.1 %shard_map.56 = (f32[2,1,256,2048]{3,2,1,0:T(8,128)}, f32[2,5024,128]{2,1,0:T(8,128)S(1)}) custom-call(f32[2,5024,128]{2,1,0:T(8,128)S(1)} %get-tuple-element.9.base, f32[2,512,128]{2,1,0:T(8,128)S(1)} %get-tuple-element.10.rows, s32[2,1,256]{2,1,0:T(1,128)S(4)} %get-tuple-element.11.index), custom_call_target="tpu_custom_call", output_to_operand_aliasing={{1}: (0, {})} | custom-call | tf_op jit(solution)/shard_map/pallas_call | solution.py:530

commit v7 on v6

--- a/solution.py
+++ b/solution.py
@@ -90,6 +90,10 @@
         return pltpu.make_async_copy(spring.at[0, :, lanes_of(cb)], spr.at[cb], spring_sem.at[cb])
 
 
+    for copy in own_copies:
+        copy.start()
+    loop(columns, lambda cb: load_field(cb).start())
+
     awaited = [there.astype(I32) for there, _ in neighbours]
     pl.semaphore_wait(barrier, sum(awaited) - early.astype(I32))
     list_copies = [
@@ -108,9 +112,6 @@
             copy.start()
 
     pl.when(late)(lambda: signal(ready, neighbours[2][1]))
-    for copy in own_copies:
-        copy.start()
-    loop(columns, lambda cb: load_field(cb).start())
     loop(columns, lambda cb: load_spring(cb).start())
 
     zero_block = jnp.zeros((fields, stride, LANES), F32)

time: 41.1 us -> 39.4 us (0.959)
  Pallas kernels: 41 us -> 39.2 us
    pallas_call x1, Pallas kernels: 37.9 us -> 36.2 us  [on_device(): pl.pallas_call(relax, out_shape=(vmem(padded, F32), vmem((fields, both, L...]
where the time goes in v7:
time: 39.4 us; the launch traced here: 39.2 us
  Pallas kernels  39.2 us (99%)
    pallas_call x1, Pallas kernels, on_device(): pl.pallas_call(relax, out_shape=(vmem(padded, F32), vmem((fields, both, L...  36.2 us
    pallas_call x1, Pallas kernels, on_device(): pl.pallas_call(finish, out_shape=(jax.ShapeDtypeStruct(displacement.shape...  3.06 us

profile of v7, /device:TPU:8, one launch (start us, length us, event | category | flops | bytes accessed | tf_op | source)
XLA Modules:
  0.0 39.2 jit_solution(9690687128776759992)
XLA Ops:
  0.0 36.2 %shard_map.55 = (f32[2,5024,128]{2,1,0:T(8,128)S(1)}, f32[2,512,128]{2,1,0:T(8,128)S(1)}, s32[2,1,256]{2,1,0:T(1,128)S(4)}) custom-call(f32[2,1,256,2048]{3,2,1,0:T(8,128)} %disp.1, f32[1,256,2048]{2,1,0:T(8,128)} %spring.1, f32[8]{0:T(128)} %table_hbm.1, s32[2,1,256]{2,1,0:T(1,128)} %blocks.1, s32[1,256]{1,0:T(1,128)} %classes.1), custom_call_target="tpu_custom_call" | custom-call | tf_op jit(solution)/shard_map/pallas_call | solution.py:503
  36.2 3.1 %shard_map.56 = (f32[2,1,256,2048]{3,2,1,0:T(8,128)}, f32[2,5024,128]{2,1,0:T(8,128)S(1)}) custom-call(f32[2,5024,128]{2,1,0:T(8,128)S(1)} %get-tuple-element.9.base, f32[2,512,128]{2,1,0:T(8,128)S(1)} %get-tuple-element.10.rows, s32[2,1,256]{2,1,0:T(1,128)S(4)} %get-tuple-element.11.index), custom_call_target="tpu_custom_call", output_to_operand_aliasing={{1}: (0, {})} | custom-call | tf_op jit(solution)/shard_map/pallas_call | solution.py:531

commit v8 on v7

--- a/solution.py
+++ b/solution.py
@@ -93,6 +93,23 @@
     for copy in own_copies:
         copy.start()
     loop(columns, lambda cb: load_field(cb).start())
+    loop(columns, lambda cb: load_spring(cb).start())
+
+    zero_block = jnp.zeros((fields, stride, LANES), F32)
+    zero_pad = jnp.zeros((fields, PAD, LANES), F32)
+    for field in (f_a, f_b):
+        for cb in range(LEFT):
+            field[:, cb * stride : (cb + 1) * stride, :] = zero_block
+        field[:, (columns + LEFT) * stride + PAD :, :] = zero_block
+        field[:, LEFT * stride : LEFT * stride + PAD, :] = zero_pad
+        loop(columns, lambda cb: field.__setitem__((slice(None), pl.ds(first_row(cb) + height, PAD), slice(None)), zero_pad))
+    for cb in range(LEFT):
+        a_ref[cb * stride : (cb + 1) * stride, :] = zero_block[0]
+    for there, side in ((has_next, 0), (has_prev, 1)):
+
+        @pl.when(jnp.logical_not(there))
+        def _(side=side):
+            received[:, :, side * matches : (side + 1) * matches, :] = jnp.zeros((ITERS, fields, matches, LANES), F32)
 
     awaited = [there.astype(I32) for there, _ in neighbours]
     pl.semaphore_wait(barrier, sum(awaited) - early.astype(I32))
@@ -112,23 +129,6 @@
             copy.start()
 
     pl.when(late)(lambda: signal(ready, neighbours[2][1]))
-    loop(columns, lambda cb: load_spring(cb).start())
-
-    zero_block = jnp.zeros((fields, stride, LANES), F32)
-    zero_pad = jnp.zeros((fields, PAD, LANES), F32)
-    for field in (f_a, f_b):
-        for cb in range(LEFT):
-            field[:, cb * stride : (cb + 1) * stride, :] = zero_block
-        field[:, (columns + LEFT) * stride + PAD :, :] = zero_block
-        field[:, LEFT * stride : LEFT * stride + PAD, :] = zero_pad
-        loop(columns, lambda cb: field.__setitem__((slice(None), pl.ds(first_row(cb) + height, PAD), slice(None)), zero_pad))
-    for cb in range(LEFT):
-        a_ref[cb * stride : (cb + 1) * stride, :] = zero_block[0]
-    for there, side in ((has_next, 0), (has_prev, 1)):
-
-        @pl.when(jnp.logical_not(there))
-        def _(side=side):
-            received[:, :, side * matches : (side + 1) * matches, :] = jnp.zeros((ITERS, fields, matches, LANES), F32)
 
     def address(block):
         return (block % columns + LEFT) * stride + PAD + block // columns

time: 39.4 us -> 39.2 us (level)
  no operation moved by 1% of the time
where the time goes in v8:
time: 39.2 us; the launch traced here: 39 us
  Pallas kernels  39 us (99%)
    pallas_call x1, Pallas kernels, on_device(): pl.pallas_call(relax, out_shape=(vmem(padded, F32), vmem((fields, both, L...  36 us
    pallas_call x1, Pallas kernels, on_device(): pl.pallas_call(finish, out_shape=(jax.ShapeDtypeStruct(displacement.shape...  3.06 us

profile of v8, /device:TPU:8, one launch (start us, length us, event | category | flops | bytes accessed | tf_op | source)
XLA Modules:
  0.0 39.0 jit_solution(7138954938659463432)
XLA Ops:
  0.0 36.0 %shard_map.55 = (f32[2,5024,128]{2,1,0:T(8,128)S(1)}, f32[2,512,128]{2,1,0:T(8,128)S(1)}, s32[2,1,256]{2,1,0:T(1,128)S(4)}) custom-call(f32[2,1,256,2048]{3,2,1,0:T(8,128)} %disp.1, f32[1,256,2048]{2,1,0:T(8,128)} %spring.1, f32[8]{0:T(128)} %table_hbm.1, s32[2,1,256]{2,1,0:T(1,128)} %blocks.1, s32[1,256]{1,0:T(1,128)} %classes.1), custom_call_target="tpu_custom_call" | custom-call | tf_op jit(solution)/shard_map/pallas_call | solution.py:503
  36.0 3.1 %shard_map.56 = (f32[2,1,256,2048]{3,2,1,0:T(8,128)}, f32[2,5024,128]{2,1,0:T(8,128)S(1)}) custom-call(f32[2,5024,128]{2,1,0:T(8,128)S(1)} %get-tuple-element.9.base, f32[2,512,128]{2,1,0:T(8,128)S(1)} %get-tuple-element.10.rows, s32[2,1,256]{2,1,0:T(1,128)S(4)} %get-tuple-element.11.index), custom_call_target="tpu_custom_call", output_to_operand_aliasing={{1}: (0, {})} | custom-call | tf_op jit(solution)/shard_map/pallas_call | solution.py:531

commit v9 on v8

--- a/solution.py
+++ b/solution.py
@@ -125,8 +125,7 @@
 
     @pl.when(has_next)
     def _():
-        for copy in list_copies:
-            copy.start()
+        list_copies[0].start()
 
     pl.when(late)(lambda: signal(ready, neighbours[2][1]))
 
@@ -191,6 +190,11 @@
 
     own_copies[0].wait()
     loop(columns, lambda cb: load_field(cb).wait())
+    @pl.when(has_next)
+    def _():
+        for copy in list_copies[1:]:
+            copy.start()
+
     for chunk in range(CHUNKS):
         gather(0, chunk * part, part, rows_of(f_a), put_sent, by_block)
         send_rows(0, 0, chunk)

time: 39.2 us -> 39.4 us (level)
  no operation moved by 1% of the time
where the time goes in v9:
time: 39.4 us; the launch traced here: 39 us
  Pallas kernels  39 us (99%)
    pallas_call x1, Pallas kernels, on_device(): pl.pallas_call(relax, out_shape=(vmem(padded, F32), vmem((fields, both, L...  36 us
    pallas_call x1, Pallas kernels, on_device(): pl.pallas_call(finish, out_shape=(jax.ShapeDtypeStruct(displacement.shape...  3.06 us

profile of v9, /device:TPU:8, one launch (start us, length us, event | category | flops | bytes accessed | tf_op | source)
XLA Modules:
  0.0 39.0 jit_solution(6825234977625508540)
XLA Ops:
  0.0 36.0 %shard_map.55 = (f32[2,5024,128]{2,1,0:T(8,128)S(1)}, f32[2,512,128]{2,1,0:T(8,128)S(1)}, s32[2,1,256]{2,1,0:T(1,128)S(4)}) custom-call(f32[2,1,256,2048]{3,2,1,0:T(8,128)} %disp.1, f32[1,256,2048]{2,1,0:T(8,128)} %spring.1, f32[8]{0:T(128)} %table_hbm.1, s32[2,1,256]{2,1,0:T(1,128)} %blocks.1, s32[1,256]{1,0:T(1,128)} %classes.1), custom_call_target="tpu_custom_call" | custom-call | tf_op jit(solution)/shard_map/pallas_call | solution.py:507
  36.0 3.1 %shard_map.56 = (f32[2,1,256,2048]{3,2,1,0:T(8,128)}, f32[2,5024,128]{2,1,0:T(8,128)S(1)}) custom-call(f32[2,5024,128]{2,1,0:T(8,128)S(1)} %get-tuple-element.9.base, f32[2,512,128]{2,1,0:T(8,128)S(1)} %get-tuple-element.10.rows, s32[2,1,256]{2,1,0:T(1,128)S(4)} %get-tuple-element.11.index), custom_call_target="tpu_custom_call", output_to_operand_aliasing={{1}: (0, {})} | custom-call | tf_op jit(solution)/shard_map/pallas_call | solution.py:535
